TPU v7x, 512 devices: a whole 4x8x8 slice. The times are simulated.
512 devices in a mesh: dp: 16 (over y, core), tensor: 8 (over z), adapter: 4 (over x).
Axes of the slice: x: 4, y: 8, z: 8, core: 2. Of those that a mesh axis runs over, the one named last changes fastest.
Arguments:
- queries: bfloat16 [4096, 8, 4, 128], P(('dp', 'tensor'), None, 'adapter'), may hold values from -125 to 125
- key_cache_rows: bfloat16 [4096, 16, 4, 128], P(('dp', 'tensor'), None, 'adapter'), may hold values from -6.5 to 6.5
- value_cache_rows: bfloat16 [4096, 16, 4, 128], P(('dp', 'tensor'), None, 'adapter'), may hold values from -6 to 6
- row_cache_length: int32 [4096], P(('dp', 'tensor')), may hold values from 2 to 16, as said below
- row_adapter_index: int32 [4096], P(('dp', 'tensor')), may hold values from 0 to 255, as said below
- adapter_storage_slot: int32 [256], replicated, may hold values from 0 to 255, as said below
- output_projection_weight: bfloat16 [8, 4, 128, 8192], P(None, 'adapter', None, 'tensor'), may hold values from -0.09375 to 0.09375
- adapter_down_weight: bfloat16 [256, 64, 8, 4, 128], P(('dp', 'tensor'), None, None, 'adapter'), may hold values from -0.09375 to 0.09375
- adapter_up_weight: bfloat16 [256, 64, 8, 1024], P(('dp', 'tensor'), None, None, 'adapter'), may hold values from -0.75 to 0.75
Outputs:
- mixed_out: bfloat16 [4096, 8192], P('dp', ('tensor', 'adapter'))
Inputs may be any that keep to these rules, and one draw needn't show every extreme that they name: `adapter_storage_slot`: a permutation; slot s lies with owner s // 2 (the index along dp+tensor) as its adapter s % 2. `row_adapter_index`: in the 32 rows of one device (aligned blocks) at most 2 rows name adapters of one owner; one owner, the same for every device, gets exactly 2 rows of every device. `row_cache_length`: 16 is reached in the rows of every device.
All inputs are finite; a program needn't handle non-finite values.
Results may differ from a plain program's by a relative error of at most 0.0064.
Values may be sent and summed in bfloat16 or wider, within the bound.
A program may use at most 64 MiB of HBM per device.

v0:
```python
import jax
import jax.numpy as jnp
from jax import lax
from jax.sharding import PartitionSpec as P


def attend(queries, key_cache_rows, value_cache_rows, row_cache_length):
    score_scale = queries.shape[-1] ** (-0.5)
    scores = (
        jnp.einsum("rgkd,rckd->rgkc", queries, key_cache_rows, preferred_element_type=jnp.float32)
        * score_scale
    )
    in_cache = (
        jnp.arange(key_cache_rows.shape[1], dtype=jnp.int32)[None, None, None, :]
        < row_cache_length[:, None, None, None]
    )
    scores = jnp.where(in_cache, scores, -1e30)
    row_max = jnp.max(scores, axis=-1, keepdims=True)
    weights = jnp.exp(scores - row_max)
    weights = (weights / jnp.sum(weights, axis=-1, keepdims=True)).astype(jnp.bfloat16)
    return jnp.einsum(
        "rgkc,rckd->rgkd", weights, value_cache_rows, preferred_element_type=jnp.float32
    ).astype(jnp.bfloat16)


def body(
    queries,
    key_cache_rows,
    value_cache_rows,
    row_cache_length,
    row_adapter_index,
    adapter_storage_slot,
    output_projection_weight,
    adapter_down_weight,
    adapter_up_weight,
):
    attention_output = attend(queries, key_cache_rows, value_cache_rows, row_cache_length)
    send_rows = attention_output.shape[0]
    features = attention_output.reshape(send_rows, -1)
    input_width = features.shape[1]
    weight_flat = output_projection_weight.reshape(input_width, output_projection_weight.shape[-1])
    partial_out = jnp.dot(
        lax.all_gather(features, "tensor", axis=0, tiled=True),
        weight_flat,
        preferred_element_type=jnp.float32,
    )
    plain_projection = lax.psum_scatter(partial_out, "adapter", scatter_dimension=1, tiled=True)
    data_groups = lax.axis_size("dp")
    tensor_groups = lax.axis_size("tensor")
    owner_count_total = data_groups * tensor_groups
    slot_capacity = max(2, 2 * send_rows // owner_count_total)
    slot_count = owner_count_total * slot_capacity
    id_match = (
        row_adapter_index[:, None]
        == jnp.arange(adapter_storage_slot.shape[0], dtype=jnp.int32)[None, :]
    )
    slot_lookup = jnp.sum(jnp.where(id_match, adapter_storage_slot[None, :], 0), axis=1)
    holding_count = adapter_down_weight.shape[0]
    adapter_rank_width = adapter_down_weight.shape[1]
    owner_of = slot_lookup // holding_count
    local_index = slot_lookup % holding_count
    owner_match = (
        owner_of[:, None] == jnp.arange(owner_count_total, dtype=jnp.int32)[None, :]
    ).astype(jnp.int32)
    earlier = jnp.cumsum(owner_match, axis=0) - owner_match
    position = jnp.sum(earlier * owner_match, axis=1)
    target = owner_of * slot_capacity + position
    routing = jnp.arange(slot_count, dtype=jnp.int32)[:, None] == target[None, :]
    routing_mat = routing.astype(jnp.bfloat16)
    packed = jnp.dot(routing_mat, features, preferred_element_type=jnp.float32).astype(jnp.bfloat16)
    packed_index = jnp.sum(jnp.where(routing, local_index[None, :] + 1, 0), axis=1) - 1
    row_place = lax.axis_index("tensor") * send_rows + jnp.arange(send_rows, dtype=jnp.int32)
    packed_place = jnp.sum(jnp.where(routing, row_place[None, :] + 1, 0), axis=1) - 1
    got_rows, got_index, got_place = (
        lax.all_to_all(
            packed.reshape(owner_count_total, slot_capacity, input_width),
            ("dp", "tensor"),
            split_axis=0,
            concat_axis=0,
            tiled=True,
        ),
        lax.all_to_all(
            packed_index.reshape(owner_count_total, slot_capacity),
            ("dp", "tensor"),
            split_axis=0,
            concat_axis=0,
            tiled=True,
        ),
        lax.all_to_all(
            packed_place.reshape(owner_count_total, slot_capacity),
            ("dp", "tensor"),
            split_axis=0,
            concat_axis=0,
            tiled=True,
        ),
    )
    got_rows = got_rows.reshape(slot_count, input_width)
    got_index = got_index.reshape(slot_count)
    got_place = got_place.reshape(slot_count)
    flat_down_maps = adapter_down_weight.reshape(holding_count * adapter_rank_width, input_width)
    shrunk = lax.dot_general(
        got_rows, flat_down_maps, (((1,), (1,)), ((), ())), preferred_element_type=jnp.float32
    )
    chosen = got_index[:, None] == jnp.arange(holding_count, dtype=jnp.int32)[None, :]
    shrunk_part = jnp.sum(
        shrunk.reshape(slot_count, holding_count, adapter_rank_width) * chosen[:, :, None], axis=1
    )
    reduced = lax.psum(shrunk_part, "adapter").astype(jnp.bfloat16)
    spread_input = (chosen[:, :, None].astype(jnp.bfloat16) * reduced[:, None, :]).reshape(
        slot_count, holding_count * adapter_rank_width
    )
    flat_up_maps = adapter_up_weight.reshape(holding_count * adapter_rank_width, -1)
    adapter_delta = jnp.dot(spread_input, flat_up_maps, preferred_element_type=jnp.float32).astype(
        jnp.bfloat16
    )
    output_width = adapter_delta.shape[1]
    column_width = output_width // tensor_groups
    returned = lax.all_to_all(
        adapter_delta.reshape(owner_count_total, slot_capacity, output_width),
        ("dp", "tensor"),
        split_axis=0,
        concat_axis=0,
        tiled=True,
    )
    returned = returned.reshape(slot_count, output_width)
    row_delta = lax.dot_general(
        routing_mat, returned, (((0,), (0,)), ((), ())), preferred_element_type=jnp.float32
    ).astype(jnp.bfloat16)
    row_delta = row_delta.reshape(send_rows, tensor_groups, column_width)
    placed = lax.all_to_all(row_delta, "tensor", split_axis=1, concat_axis=0, tiled=True)
    placed = placed.reshape(-1, column_width)
    return (plain_projection + placed.astype(jnp.float32)).astype(jnp.bfloat16)


def solution(mesh):
    return jax.shard_map(
        body,
        mesh=mesh,
        in_specs=(
            P(("dp", "tensor"), None, "adapter", None),
            P(("dp", "tensor"), None, "adapter", None),
            P(("dp", "tensor"), None, "adapter", None),
            P(("dp", "tensor")),
            P(("dp", "tensor")),
            P(),
            P(None, "adapter", None, "tensor"),
            P(("dp", "tensor"), None, None, "adapter", None),
            P(("dp", "tensor"), None, None, "adapter"),
        ),
        out_specs=P("dp", ("tensor", "adapter")),
        check_vma=False,
    )
```

profile of v0, /device:TPU:1, one launch (start us, length us, event | category | flops | bytes accessed | tf_op | source)
XLA Modules:
  0.0 172.7 jit_solution(10845552292885122140)
XLA Ops:
  6.5 0.0 copy-start
  6.5 1.0 select_reduce_fusion.1
  7.6 0.1 fusion.13
  7.6 0.1 reduce_window_sum.11
  7.7 0.2 select_reduce_fusion.2
  7.9 0.1 select_reduce_fusion
  8.0 0.8 sub.28
  8.8 18.4 %all-to-all-start = ((s32[128,1,2]{2,1,0:T(1,128)}), s32[128,1,2]{2,1,0:T(1,128)S(1)}, u32[]{:S(2)}, u32[]{:S(2)}) async-start(s32[128,1,2]{2,1,0:T(1,128)} %bitcast.10), calls=%async_computation.1 | async-start | bytes 131072 | tf_op jit(solution)/shard_map/all_to_all | solution.py:82
  27.2 0.7 iota_compare_fusion.5
  27.9 1.2 fusion.17
  29.1 0.0 copy-start.1
  29.1 0.2 fusion.7
  29.3 1.2 convolution_convert_fusion.3
  30.5 0.4 convolution_convert_fusion.2
  30.9 1.0 reshape.225
  31.9 6.5 %all-to-all-done = s32[128,1,2]{2,1,0:T(1,128)S(1)} async-done(((s32[128,1,2]{2,1,0:T(1,128)}), s32[128,1,2]{2,1,0:T(1,128)S(1)}, u32[]{:S(2)}, u32[]{:S(2)}) %all-to-all-start) | async-done | bytes 1056 | tf_op jit(solution)/shard_map/all_to_all | solution.py:82
  38.4 7.2 %all-to-all-start.1 = ((bf16[128,2,1024]{2,1,0:T(2,128)(2,1)}), bf16[128,2,1024]{2,1,0:T(2,128)(2,1)S(1)}, u32[]{:S(2)}, u32[]{:S(2)}) async-start(bf16[128,2,1024]{2,1,0:T(2,128)(2,1)} %reshape.225), calls=%async_computation.2 | async-start | bytes 1048576 | tf_op jit(solution)/shard_map/all_to_all | solution.py:75
  45.6 1.1 dot_general.27
  46.7 0.0 copy-done.1
  46.7 0.9 copy.19
  47.6 0.5 broadcast.190
  48.1 0.8 reduce.5
  48.9 0.1 eq.72
  49.1 17.4 %all-to-all-done.1 = bf16[128,2,1024]{2,1,0:T(2,128)(2,1)S(1)} async-done(((bf16[128,2,1024]{2,1,0:T(2,128)(2,1)}), bf16[128,2,1024]{2,1,0:T(2,128)(2,1)S(1)}, u32[]{:S(2)}, u32[]{:S(2)}) %all-to-all-start.1) | async-done | bytes 524320 | tf_op jit(solution)/shard_map/all_to_all | solution.py:75
  66.5 0.2 reshape.233
  66.7 0.3 fusion.1
  67.0 13.8 %psum.7 = bf16[256,64]{0,1:T(8,128)(2,1)S(1)} all-reduce(f32[256,64]{0,1:T(8,128)S(1)} %fusion.1), channel_id=1, replica_groups=mesh['dp'=16,'tensor'=8,'adapter'=4] {'adapter'}, use_global_device_ids=true, to_apply=%region_8.9 | all-reduce | flops 16384 | bytes 98304 | tf_op jit(solution)/shard_map/psum | solution.py:108
  80.8 1.5 convolution_convert_fusion
  82.3 1.5 reshape.228
  83.8 8.8 %all-to-all-start.2 = ((bf16[128,2,2048]{2,1,0:T(2,128)(2,1)}), bf16[128,2,2048]{2,1,0:T(2,128)(2,1)S(1)}, u32[]{:S(2)}, u32[]{:S(2)}) async-start(bf16[128,2,2048]{2,1,0:T(2,128)(2,1)} %reshape.228), calls=%async_computation.3 | async-start | bytes 2097152 | tf_op jit(solution)/shard_map/all_to_all | solution.py:118
  92.6 0.0 reduce-scatter.2.cloned.1.call-start
  92.7 36.4 %all_gather.3 = bf16[256,1024]{1,0:T(8,128)(2,1)S(1)} all-gather(bf16[32,1024]{1,0:T(8,128)(2,1)S(1)} %bitcast.72), channel_id=1, replica_groups=mesh['dp'=16,'tensor'=8,'adapter'=4] {'tensor'}, dimensions={0}, use_global_device_ids=true | all-gather | bytes 589824 | tf_op jit(solution)/shard_map/all_gather | solution.py:43
  129.1 0.0 copy-done
  129.1 1.7 fusion.18
  130.8 0.0 reduce-scatter.2.cloned.1.call-update
  130.8 0.0 all-to-all-done.2
  130.8 1.3 reshape.229
  132.1 1.5 convolution_convert_fusion.1
  133.7 12.2 %all_to_all.25 = bf16[32,8,256]{2,0,1:T(8,128)(2,1)S(1)} all-to-all(bf16[32,8,256]{2,0,1:T(8,128)(2,1)S(1)} %bitcast.70), channel_id=1, replica_groups=mesh['dp'=16,'tensor'=8,'adapter'=4] {'tensor'}, dimensions={1} | all-to-all | bytes 262144 | tf_op jit(solution)/shard_map/all_to_all | solution.py:130
  145.8 18.4 %reduce-scatter.2.cloned.1.call-done = f32[256,256]{1,0:T(8,128)} async-done(((f32[256,1024]{1,0:T(8,128)}), f32[256,256]{1,0:T(8,128)}) %reduce-scatter.2.cloned.1.call-update) | async-done | bytes 262160 | tf_op jit(solution)/shard_map/reduce_scatter | solution.py:47
  164.2 1.6 fusion.4
  (8 shorter events, 0.1 us)
Async XLA Ops:
  6.5 122.6 %copy-start = (bf16[8,1,128,1024]{3,2,1,0:T(8,128)(2,1)S(1)}, bf16[8,1,128,1024]{3,2,1,0:T(8,128)(2,1)}, u32[]{:S(2)}) copy-start(bf16[8,1,128,1024]{3,2,1,0:T(8,128)(2,1)} %param.15) | copy-start | bytes 6291460
  8.8 29.6 %all-to-all-start = ((s32[128,1,2]{2,1,0:T(1,128)}), s32[128,1,2]{2,1,0:T(1,128)S(1)}, u32[]{:S(2)}, u32[]{:S(2)}) async-start(s32[128,1,2]{2,1,0:T(1,128)} %bitcast.10), calls=%async_computation.1 | async-start | bytes 131072 | tf_op jit(solution)/shard_map/all_to_all | solution.py:82
  29.1 17.6 %copy-start.1 = (bf16[2,64,8,256]{3,2,1,0:T(8,128)(2,1)S(1)}, bf16[2,64,8,256]{3,2,1,0:T(8,128)(2,1)}, u32[]{:S(2)}) copy-start(bf16[2,64,8,256]{3,2,1,0:T(8,128)(2,1)} %param.17) | copy-start | bytes 1572868
  38.4 28.1 %all-to-all-start.1 = ((bf16[128,2,1024]{2,1,0:T(2,128)(2,1)}), bf16[128,2,1024]{2,1,0:T(2,128)(2,1)S(1)}, u32[]{:S(2)}, u32[]{:S(2)}) async-start(bf16[128,2,1024]{2,1,0:T(2,128)(2,1)} %reshape.225), calls=%async_computation.2 | async-start | bytes 1048576 | tf_op jit(solution)/shard_map/all_to_all | solution.py:75
  83.8 47.0 %all-to-all-start.2 = ((bf16[128,2,2048]{2,1,0:T(2,128)(2,1)}), bf16[128,2,2048]{2,1,0:T(2,128)(2,1)S(1)}, u32[]{:S(2)}, u32[]{:S(2)}) async-start(bf16[128,2,2048]{2,1,0:T(2,128)(2,1)} %reshape.228), calls=%async_computation.3 | async-start | bytes 2097152 | tf_op jit(solution)/shard_map/all_to_all | solution.py:118
  92.6 71.6 %reduce-scatter.2.cloned.1.call-start = ((), (), s32[]{:S(2)}) async-start(), calls=%async_computation.5 | async-start | bytes 1310720 | tf_op jit(solution)/shard_map/reduce_scatter | solution.py:47
Sparse Core Ops, SparseCore 0:
  131.0 33.2 reduce-scatter.1
where the time goes:
time: 174 us; the launch traced here: 173 us
  blocking collectives  62.3 us (36%)
  waiting for transfers between devices  42.4 us (24%)
  starting transfers between devices  34.4 us (20%)
  between operations  13.6 us (8%)
  matrix products  7.76 us (4%)
  local copies, waits for them, and re-layouts  7.42 us (4%)
  other arithmetic  4.81 us (3%)
    all_gather x1, blocking collectives, body(): lax.all_gather(features, 'tensor', axis=0, tiled=True)  36.4 us
    all_to_all x1, starting transfers between devices, body(): lax.all_to_all(packed_index.reshape(owner_count_total, slot_capacity), ('...  18.4 us
    reduce_scatter x1, waiting for transfers between devices, body(): lax.psum_scatter(partial_out, 'adapter', scatter_dimension=1, tiled=True)  18.4 us
    all_to_all x1, waiting for transfers between devices, body(): lax.all_to_all(packed.reshape(owner_count_total, slot_capacity, input_wid...  17.4 us
    psum x1, blocking collectives, body(): reduced = lax.psum(shrunk_part, 'adapter').astype(jnp.bfloat16)  13.8 us
    all_to_all x1, blocking collectives, body(): lax.all_to_all(row_delta, 'tensor', split_axis=1, concat_axis=0, tiled=True)  12.2 us
    all_to_all x1, starting transfers between devices, body(): lax.all_to_all(adapter_delta.reshape(owner_count_total, slot_capacity, ou...  8.81 us
    all_to_all x1, starting transfers between devices, body(): lax.all_to_all(packed.reshape(owner_count_total, slot_capacity, input_wid...  7.16 us
  transfers between devices with their start and end apart: 4, of which 3 were waited for; matrix products, arithmetic and copies ran while one was open for 7% of the time, Pallas kernels for 0%

commit v1 on v0

v1 whole, which is shorter than its diff:
```python
import functools

import jax
import jax.numpy as jnp
from jax import lax
from jax.experimental import pallas as pl
from jax.experimental.pallas import tpu as pltpu
from jax.sharding import PartitionSpec as P

MESH = pl.DeviceIdType.MESH
CAP = 2
F32 = jnp.float32
BF16 = jnp.bfloat16


def iota(shape, dim):
    return lax.broadcasted_iota(jnp.int32, shape, dim)


def dot(a, b):
    return jnp.dot(a, b, preferred_element_type=F32)


def dot_t(a, b):
    return lax.dot_general(a, b, (((1,), (1,)), ((), ())), preferred_element_type=F32)


def regroup(rows, groups):
    n = rows * groups
    out, into = iota((n, n), 0), iota((n, n), 1)
    return jnp.where(into == (out % rows) * groups + out // rows, 1.0, 0.0).astype(BF16)


def column_of(row, n):
    return jnp.sum(jnp.where(iota((n, n), 0) == iota((n, n), 1), row, 0.0), axis=1, keepdims=True)


def row_of(column, n):
    return jnp.sum(jnp.where(iota((n, n), 0) == iota((n, n), 1), column, 0.0), axis=0, keepdims=True)


def attend(q_ref, k_ref, v_ref, length_row, rows, groups, cache):
    per = 128 // cache if rows * cache > 128 else rows
    width = per * cache
    lengths = jnp.sum(
        jnp.where(iota((rows * groups, rows), 0) // groups == iota((rows * groups, rows), 1), length_row, 0.0),
        axis=1,
        keepdims=True,
    )
    outs = []
    for first in range(0, rows, per):
        q = q_ref[first * groups : (first + per) * groups, :]
        k = k_ref[first * cache : (first + per) * cache, :]
        v = v_ref[first * cache : (first + per) * cache, :]
        shape = (per * groups, width)
        lane = iota(shape, 1)
        live = (iota(shape, 0) // groups == lane // cache) & (
            (lane % cache).astype(F32) < lengths[first * groups : (first + per) * groups, :]
        )
        scores = jnp.where(live, dot_t(q, k) * (q.shape[-1] ** -0.5), -1e30)
        weights = jnp.exp(scores - jnp.max(scores, axis=1, keepdims=True))
        weights = jnp.where(live, weights, 0.0)
        weights = (weights / jnp.sum(weights, axis=1, keepdims=True)).astype(BF16)
        outs.append(dot(weights, v).astype(BF16))
    return jnp.concatenate(outs, axis=0)


def kernel(
    nd, nt, na, groups, cache, holding,
    q_ref, k_ref, v_ref, len_ref, idx_ref, slot_ref, w_hbm, down_ref, up_ref, out_ref,
    xg, pk, rx, w_ref, downp, upp, upg, btx, brx, acc, ptx, prx, redg, ret_tx, ret_rx,
    w_sem, z_send, z_recv, u_send, u_recv, y_send, y_recv, b_send, b_recv, p_send, p_recv,
    r_send, r_recv, f_send, f_recv,
):
    d, t, a = lax.axis_index("dp"), lax.axis_index("tensor"), lax.axis_index("adapter")
    rows = q_ref.shape[0] // groups
    feat = groups * 128
    spots = nt * CAP
    slots = nd * spots
    rank2 = 128
    all_rows = nt * rows
    cols = acc.shape[1]

    def z_dev(k):
        return (d, lax.rem(t + k, nt), a)

    def y_dev(k):
        return (lax.rem(d + k, nd), t, a)

    def x_dev(k):
        return (d, t, lax.rem(a + k, na))

    w_copy = pltpu.make_async_copy(w_hbm, w_ref, w_sem)
    w_copy.start()
    barrier = pltpu.get_barrier_semaphore()
    for n, dev in ((nt, z_dev), (nd, y_dev), (na, x_dev)):
        def greet(k, c, dev=dev):
            pl.semaphore_signal(barrier, inc=1, device_id=dev(k), device_id_type=MESH)
            return c
        lax.fori_loop(1, n, greet, 0)

    idx_col = column_of(idx_ref[...].astype(F32), rows)
    table = slot_ref.shape[1]
    slot_col = jnp.sum(
        jnp.where(idx_col == iota((rows, table), 1).astype(F32), slot_ref[...].astype(F32), 0.0),
        axis=1, keepdims=True,
    )
    owner_col = jnp.floor(slot_col * (1.0 / holding))
    local_col = slot_col - holding * owner_col
    owner_row = row_of(owner_col, rows)
    earlier = (owner_row == owner_col) & (iota((rows, rows), 1) < iota((rows, rows), 0))
    pos_col = jnp.sum(jnp.where(earlier, 1.0, 0.0), axis=1, keepdims=True)
    code = owner_col * CAP + pos_col + 1.0
    tags = jnp.where((iota((rows, rank2), 1) // (rank2 // holding)).astype(F32) == local_col, code, 0.0)

    att = attend(q_ref, k_ref, v_ref, len_ref[...].astype(F32), rows, groups, cache)
    swap = regroup(rows, groups)
    att = dot(swap, att).astype(BF16)
    mine = pl.ds(pl.multiple_of(t * rows, rows), rows)
    for g in range(groups):
        xg[mine, g * 128 : (g + 1) * 128] = att[g * rows : (g + 1) * rows, :]
    xg[mine, feat : feat + rank2] = tags.astype(BF16)

    pl.semaphore_wait(barrier, (nt - 1) + (nd - 1) + (na - 1))

    def z_copy(k, block):
        part = xg.at[pl.ds(pl.multiple_of(block * rows, rows), rows)]
        return pltpu.make_async_remote_copy(
            src_ref=part, dst_ref=part, send_sem=z_send.at[k], recv_sem=z_recv.at[k],
            device_id=z_dev(k), device_id_type=MESH)

    def z_start(k, c):
        z_copy(k, t).start()
        return c
    lax.fori_loop(1, nt, z_start, 0)

    step = 256 // groups
    swap_w = regroup(step, groups)
    for b in range(holding * 64 // step):
        part = slice(b * step * groups, (b + 1) * step * groups)
        up = dot(swap_w, up_ref[part, :]).astype(BF16)
        for g in range(nt):
            upp[g, b * step : (b + 1) * step, :] = up[g * step : (g + 1) * step, :]

    def u_copy(k):
        return pltpu.make_async_remote_copy(
            src_ref=upp.at[lax.rem(t + k, nt)], dst_ref=upg.at[t], send_sem=u_send.at[k],
            recv_sem=u_recv.at[k], device_id=z_dev(k), device_id_type=MESH)

    def u_start(k, c):
        u_copy(k).start()
        return c
    lax.fori_loop(1, nt, u_start, 0)
    upg[t] = upp[t]
    for b in range(holding * 64 // step):
        part = slice(b * step * groups, (b + 1) * step * groups)
        down = dot(swap_w, down_ref[part, :]).astype(BF16)
        for g in range(groups):
            downp[b * step : (b + 1) * step, g * 128 : (g + 1) * 128] = down[g * step : (g + 1) * step, :]

    def z_wait(k, c):
        z_copy(k, lax.rem(t - k + nt, nt)).wait_recv()
        return c
    lax.fori_loop(1, nt, z_wait, 0)

    tag = xg[:, feat : feat + rank2].astype(F32)
    codes = tag[:, 0:1] + tag[:, rank2 // 2 : rank2 // 2 + 1] - 1.0
    owners = jnp.floor(codes * (1.0 / CAP))
    pos = codes - CAP * owners
    owner_d = jnp.floor(owners * (1.0 / nt))
    owner_t = owners - nt * owner_d
    place = (iota((all_rows, 1), 0) // rows).astype(F32) * CAP + pos
    target = jnp.where(owner_t == t.astype(F32), owner_d * spots + place, -1.0)
    target_row = row_of(target, all_rows)
    route = jnp.where(iota((slots, all_rows), 0).astype(F32) == target_row, 1.0, 0.0).astype(BF16)
    pk[...] = dot(route, xg[...]).astype(BF16)

    def spot(block):
        return pl.ds(pl.multiple_of(block * spots, spots), spots)

    def y_copy(k):
        return pltpu.make_async_remote_copy(
            src_ref=pk.at[spot(lax.rem(d + k, nd))], dst_ref=rx.at[spot(d)], send_sem=y_send.at[k],
            recv_sem=y_recv.at[k], device_id=y_dev(k), device_id_type=MESH)

    def y_start(k, c):
        y_copy(k).start()
        return c
    lax.fori_loop(1, nd, y_start, 0)
    rx[spot(d), :] = pk[spot(d), :]

    w_copy.wait()
    x = xg[:, :feat]

    def b_copy(k):
        return pltpu.make_async_remote_copy(
            src_ref=btx.at[k], dst_ref=brx.at[k], send_sem=b_send.at[k],
            recv_sem=b_recv.at[k], device_id=x_dev(k), device_id_type=MESH)
    for k in range(1, na):
        part = pl.ds(pl.multiple_of(lax.rem(a + k, na) * cols, cols), cols)
        btx[k] = dot(x, w_ref[:, part]).astype(BF16)
        b_copy(k).start()
    acc[...] = dot(x, w_ref[:, pl.ds(pl.multiple_of(a * cols, cols), cols)])

    def y_wait(k, c):
        y_copy(k).wait_recv()
        return c
    lax.fori_loop(1, nd, y_wait, 0)

    shrunk = dot_t(rx[:, :feat], downp[...])
    shrunk = jnp.where(rx[:, feat : feat + rank2].astype(F32) > 0.0, shrunk, 0.0)
    ptx[...] = shrunk.astype(BF16)

    def p_copy(k):
        return pltpu.make_async_remote_copy(
            src_ref=ptx, dst_ref=prx.at[k], send_sem=p_send.at[k],
            recv_sem=p_recv.at[k], device_id=x_dev(k), device_id_type=MESH)
    for k in range(1, na):
        p_copy(k).start()
    for k in range(1, na):
        p_copy(k).wait_recv()
        shrunk = shrunk + prx[k].astype(F32)
    redg[t] = shrunk.astype(BF16)

    def r_copy(k):
        return pltpu.make_async_remote_copy(
            src_ref=redg.at[t], dst_ref=redg.at[t], send_sem=r_send.at[k],
            recv_sem=r_recv.at[k], device_id=z_dev(k), device_id_type=MESH)

    def r_start(k, c):
        r_copy(k).start()
        return c
    lax.fori_loop(1, nt, r_start, 0)

    def r_wait(k, c):
        r_copy(k).wait_recv()
        u_copy(k).wait_recv()
        return c
    lax.fori_loop(1, nt, r_wait, 0)
    for g in range(nt):
        grown = dot(redg[g], upg[g]).astype(BF16)
        ret_tx[:, g, :, :] = grown.reshape(nd, spots, cols)

    def f_copy(k):
        return pltpu.make_async_remote_copy(
            src_ref=ret_tx.at[lax.rem(d + k, nd)], dst_ref=ret_rx.at[d], send_sem=f_send.at[k],
            recv_sem=f_recv.at[k], device_id=y_dev(k), device_id_type=MESH)

    def f_start(k, c):
        f_copy(k).start()
        return c
    lax.fori_loop(1, nd, f_start, 0)
    ret_rx[d] = ret_tx[d]

    for k in range(1, na):
        b_copy(k).wait_recv()
        acc[...] += brx[k].astype(F32)
    target = owners * spots + place

    def f_wait(k, c):
        f_copy(k).wait_recv()
        return c
    lax.fori_loop(1, nd, f_wait, 0)
    total = acc[...]
    span = nt * spots
    for g in range(nd):
        pick = jnp.where((iota((all_rows, span), 1) + g * span).astype(F32) == target, 1.0, 0.0).astype(BF16)
        total = total + dot(pick, ret_rx[g].reshape(span, cols))
    out_ref[...] = total.astype(BF16)

    def drain_z(k, c):
        z_copy(k, t).wait_send()
        u_copy(k).wait_send()
        r_copy(k).wait_send()
        return c
    lax.fori_loop(1, nt, drain_z, 0)

    def drain_y(k, c):
        y_copy(k).wait_send()
        f_copy(k).wait_send()
        return c
    lax.fori_loop(1, nd, drain_y, 0)
    for k in range(1, na):
        b_copy(k).wait_send()
        p_copy(k).wait_send()


def body(sizes, q, kc, vc, lengths, index, table, w, down, up):
    nd, nt, na = sizes
    rows, groups, _, width = q.shape
    cache = kc.shape[1]
    holding, rank = down.shape[0], down.shape[1]
    feat = groups * width
    columns = w.shape[-1]
    cols = columns // na
    spots = nt * CAP
    slots = nd * spots
    wide = feat + holding * rank
    hr = holding * rank
    vmem = pl.BlockSpec(memory_space=pltpu.VMEM)
    dma = pltpu.SemaphoreType.DMA
    return pl.pallas_call(
        functools.partial(kernel, nd, nt, na, groups, cache, holding),
        out_shape=jax.ShapeDtypeStruct((nt * rows, cols), BF16),
        in_specs=[vmem] * 6 + [pl.BlockSpec(memory_space=pl.ANY)] + [vmem] * 2,
        out_specs=vmem,
        scratch_shapes=[
            pltpu.VMEM((nt * rows, wide), BF16),
            pltpu.VMEM((slots, wide), BF16),
            pltpu.VMEM((slots, wide), BF16),
            pltpu.VMEM((feat, columns), BF16),
            pltpu.VMEM((hr, feat), BF16),
            pltpu.VMEM((nt, hr, cols), BF16),
            pltpu.VMEM((nt, hr, cols), BF16),
            pltpu.VMEM((na, nt * rows, cols), BF16),
            pltpu.VMEM((na, nt * rows, cols), BF16),
            pltpu.VMEM((nt * rows, cols), F32),
            pltpu.VMEM((slots, hr), BF16),
            pltpu.VMEM((na, slots, hr), BF16),
            pltpu.VMEM((nt, slots, hr), BF16),
            pltpu.VMEM((nd, nt, spots, cols), BF16),
            pltpu.VMEM((nd, nt, spots, cols), BF16),
            dma,
            dma((nt,)), dma((nt,)), dma((nt,)), dma((nt,)),
            dma((nd,)), dma((nd,)),
            dma((na,)), dma((na,)), dma((na,)), dma((na,)),
            dma((nt,)), dma((nt,)),
            dma((nd,)), dma((nd,)),
        ],
        compiler_params=pltpu.CompilerParams(
            collective_id=0, has_side_effects=True, vmem_limit_bytes=40 * 1024 * 1024
        ),
    )(
        q.reshape(rows * groups, width),
        kc.reshape(rows * cache, width),
        vc.reshape(rows * cache, width),
        lengths.reshape(1, rows),
        index.reshape(1, rows),
        table.reshape(1, -1),
        w.reshape(feat, columns),
        down.reshape(hr * groups, width),
        up.reshape(hr * nt, cols),
    )


def solution(mesh):
    sizes = tuple(mesh.shape[name] for name in ("dp", "tensor", "adapter"))
    return jax.shard_map(
        functools.partial(body, sizes),
        mesh=mesh,
        in_specs=(
            P(("dp", "tensor"), None, "adapter", None),
            P(("dp", "tensor"), None, "adapter", None),
            P(("dp", "tensor"), None, "adapter", None),
            P(("dp", "tensor")),
            P(("dp", "tensor")),
            P(),
            P(None, "adapter", None, "tensor"),
            P(("dp", "tensor"), None, None, "adapter", None),
            P(("dp", "tensor"), None, None, "adapter"),
        ),
        out_specs=P("dp", ("tensor", "adapter")),
        check_vma=False,
    )
```

time: 174 us -> 102 us (0.59)
  Pallas kernels: 0 us -> 91.2 us
  blocking collectives: 62.3 us -> 0 us
  waiting for transfers between devices: 42.4 us -> 0 us
  starting transfers between devices: 34.4 us -> 0 us
  between operations: 13.6 us -> 0.02 us
  matrix products: 7.76 us -> 0 us
  other arithmetic: 4.81 us -> 0 us
    pallas_call x0 -> x1, Pallas kernels: none -> 91.2 us  [body(): pl.pallas_call(functools.partial(kernel, nd, nt, na, groups, cache, holdi...]
    all_gather x1 -> x0, blocking collectives: 36.4 us -> none  [body(): lax.all_gather(features, 'tensor', axis=0, tiled=True)]
    all_to_all x3 -> x0, starting transfers between devices: 34.4 us -> none  [the longest x1 18.4 us: body(): lax.all_to_all(packed_index.reshape(owner_count_total, slot_capacity), ('...]
    all_to_all x3 -> x0, waiting for transfers between devices: 24 us -> none  [the longest x1 17.4 us: body(): lax.all_to_all(packed.reshape(owner_count_total, slot_capacity, input_wid...]
    reduce_scatter x1 -> x0, waiting for transfers between devices: 18.4 us -> none  [body(): lax.psum_scatter(partial_out, 'adapter', scatter_dimension=1, tiled=True)]
    psum x1 -> x0, blocking collectives: 13.8 us -> none  [body(): reduced = lax.psum(shrunk_part, 'adapter').astype(jnp.bfloat16)]
    all_to_all x1 -> x0, blocking collectives: 12.2 us -> none  [body(): lax.all_to_all(row_delta, 'tensor', split_axis=1, concat_axis=0, tiled=True)]
    unnamed x6 -> x19, local copies, waits for them, and re-layouts: 0.95 us -> 8.87 us
  transfers between devices with their start and end apart: 4 -> 0, of which waited for: 3 -> 0; matrix products, arithmetic and copies ran while one was open for 7% -> 0% of each run, Pallas kernels for 0% -> 0%
where the time goes in v1:
time: 102 us; the launch traced here: 100 us
  Pallas kernels  91.2 us (89%)
  local copies, waits for them, and re-layouts  8.87 us (9%)
    pallas_call x1, Pallas kernels, body(): pl.pallas_call(functools.partial(kernel, nd, nt, na, groups, cache, holdi...  91.2 us
    unnamed x19, local copies, waits for them, and re-layouts  8.87 us

profile of v1, /device:TPU:1, one launch (start us, length us, event | category | flops | bytes accessed | tf_op | source)
XLA Modules:
  0.0 100.1 jit_solution(17710606253781913906)
XLA Ops:
  0.0 0.0 copy-start
  0.0 1.6 %copy-done = bf16[8,1,128,1024]{3,2,1,0:T(8,128)(2,1)S(1)} copy-done((bf16[8,1,128,1024]{3,2,1,0:T(8,128)(2,1)S(1)}, bf16[8,1,128,1024]{3,2,1,0:T(8,128)(2,1)}, u32[]{:S(2)}) %copy-start) | copy-done | bytes 2097176
  1.6 0.0 copy-start.1
  1.6 1.0 %copy-done.1 = bf16[2,64,8,256]{3,2,1,0:T(8,128)(2,1)S(1)} copy-done((bf16[2,64,8,256]{3,2,1,0:T(8,128)(2,1)S(1)}, bf16[2,64,8,256]{3,2,1,0:T(8,128)(2,1)}, u32[]{:S(2)}) %copy-start.1) | copy-done | bytes 524312
  2.6 0.0 copy-start.2
  2.6 0.9 copy-done.2
  3.6 0.0 copy-start.3
  3.6 0.9 copy-done.3
  4.5 0.0 copy-start.4
  4.5 0.9 copy-done.4
  5.4 0.0 copy-start.5
  5.4 0.8 copy-done.5
  6.2 0.0 copy-start.6
  6.2 0.7 copy-done.6
  6.9 0.0 copy-start.7
  6.9 0.7 copy-done.7
  7.6 0.0 copy-start.8
  7.6 0.7 copy-done.8
  8.2 91.2 %shard_map.91 = bf16[256,256]{1,0:T(8,128)(2,1)S(1)} custom-call(bf16[256,128]{1,0:T(8,128)(2,1)S(1)} %bitcast.14, bf16[512,128]{1,0:T(8,128)(2,1)S(1)} %bitcast.12, bf16[512,128]{1,0:T(8,128)(2,1)S(1)} %bitcast.13, s32[1,32]{1,0:T(1,128)S(1)} %bitcast.16, s32[1,32]{1,0:T(1,128)S(1)} %bitcast.17, s32[1,256]{1,0:T(1,128)S(1)} %bitcast.15, ...), custom_call_target="tpu_custom_call" | custom-call | tf_op jit(solution)/shard_map/pallas_call | solution.py:302
  99.5 0.7 copy.11
Async XLA Ops:
  0.0 1.6 %copy-start = (bf16[8,1,128,1024]{3,2,1,0:T(8,128)(2,1)S(1)}, bf16[8,1,128,1024]{3,2,1,0:T(8,128)(2,1)}, u32[]{:S(2)}) copy-start(bf16[8,1,128,1024]{3,2,1,0:T(8,128)(2,1)} %param.15) | copy-start | bytes 6291460
  1.6 1.0 %copy-start.1 = (bf16[2,64,8,256]{3,2,1,0:T(8,128)(2,1)S(1)}, bf16[2,64,8,256]{3,2,1,0:T(8,128)(2,1)}, u32[]{:S(2)}) copy-start(bf16[2,64,8,256]{3,2,1,0:T(8,128)(2,1)} %param.17) | copy-start | bytes 1572868
  2.6 0.9 copy-start.2
  3.6 0.9 copy-start.3
  4.5 0.9 copy-start.4
  5.4 0.8 copy-start.5
  6.2 0.7 copy-start.6
  6.9 0.7 copy-start.7
  7.6 0.7 copy-start.8

commit v2 on v1

v2 whole, which is shorter than its diff:
```python
import functools

import jax
import jax.numpy as jnp
from jax import lax
from jax.experimental import pallas as pl
from jax.experimental.pallas import tpu as pltpu
from jax.sharding import PartitionSpec as P

MESH = pl.DeviceIdType.MESH
CAP = 2
F32 = jnp.float32
BF16 = jnp.bfloat16


def iota(shape, dim):
    return lax.broadcasted_iota(jnp.int32, shape, dim)


def dot(a, b):
    return jnp.dot(a, b, preferred_element_type=F32)


def dot_t(a, b):
    return lax.dot_general(a, b, (((1,), (1,)), ((), ())), preferred_element_type=F32)


def regroup(rows, groups):
    n = rows * groups
    out, into = iota((n, n), 0), iota((n, n), 1)
    return jnp.where(into == (out % rows) * groups + out // rows, 1.0, 0.0).astype(BF16)


def column_of(row, n):
    return jnp.sum(jnp.where(iota((n, n), 0) == iota((n, n), 1), row, 0.0), axis=1, keepdims=True)


def row_of(column, n):
    return jnp.sum(jnp.where(iota((n, n), 0) == iota((n, n), 1), column, 0.0), axis=0, keepdims=True)


def attend(q_ref, k_ref, v_ref, length_row, rows, groups, cache):
    per = 128 // cache if rows * cache > 128 else rows
    width = per * cache
    lengths = jnp.sum(
        jnp.where(iota((rows * groups, rows), 0) // groups == iota((rows * groups, rows), 1), length_row, 0.0),
        axis=1,
        keepdims=True,
    )
    outs = []
    for first in range(0, rows, per):
        q = q_ref[first * groups : (first + per) * groups, :]
        k = k_ref[first * cache : (first + per) * cache, :]
        v = v_ref[first * cache : (first + per) * cache, :]
        shape = (per * groups, width)
        lane = iota(shape, 1)
        live = (iota(shape, 0) // groups == lane // cache) & (
            (lane % cache).astype(F32) < lengths[first * groups : (first + per) * groups, :]
        )
        scores = jnp.where(live, dot_t(q, k) * (q.shape[-1] ** -0.5), -1e30)
        weights = jnp.exp(scores - jnp.max(scores, axis=1, keepdims=True))
        weights = jnp.where(live, weights, 0.0)
        weights = (weights / jnp.sum(weights, axis=1, keepdims=True)).astype(BF16)
        outs.append(dot(weights, v).astype(BF16))
    return jnp.concatenate(outs, axis=0)


def order_of(chips):
    near = [0]
    for j in range(1, chips // 2 + 1):
        near += [j] if 2 * j == chips else [j, chips - j]
    cuts = sorted({0, min(3, chips), min(5, chips), chips})
    return near, [(2 * lo, 2 * hi) for lo, hi in zip(cuts[:-1], cuts[1:])]


def kernel(
    nd, nt, na, groups, cache, holding,
    q_hbm, k_hbm, v_hbm, len_hbm, idx_hbm, slot_hbm, w_hbm, down_hbm, up_hbm, out_ref,
    q_ref, k_ref, v_ref, len_ref, idx_ref, slot_ref, down_ref, up_ref,
    xg, pk, rx, w_ref, downp, upp, upg, btx, brx, acc, ptx, prx, redg, ret_tx, ret_rx,
    in_sem, z_send, z_recv, u_send, u_recv, y_send, y_recv, b_send, b_recv, p_send, p_recv,
    r_send, r_recv, f_send, f_recv,
):
    d, t, a = lax.axis_index("dp"), lax.axis_index("tensor"), lax.axis_index("adapter")
    rows = q_ref.shape[0] // groups
    feat = groups * 128
    spots = nt * CAP
    slots = nd * spots
    half = 64
    lanes = 2 * half
    all_rows = nt * rows
    cols = acc.shape[1]
    chips = nd // 2
    near, runs = order_of(chips)
    chip, core = d // 2, d % 2

    def dp_at(m):
        return 2 * lax.rem(chip + near[m // 2], chips) + lax.rem(core + m % 2, 2)

    def back(m):
        return 2 * near.index((chips - near[m // 2]) % chips) + m % 2

    def z_dev(k):
        return (d, lax.rem(t + k, nt), a)

    def x_dev(k):
        return (d, t, lax.rem(a + k, na))

    fetches = [
        pltpu.make_async_copy(src, dst, in_sem.at[n])
        for n, (src, dst) in enumerate((
            (idx_hbm, idx_ref), (slot_hbm, slot_ref), (len_hbm, len_ref), (q_hbm, q_ref), (k_hbm, k_ref),
            (v_hbm, v_ref), (up_hbm, up_ref), (down_hbm, down_ref), (w_hbm, w_ref)))
    ]
    for fetch in fetches:
        fetch.start()
    barrier = pltpu.get_barrier_semaphore()

    def greet_z(k, c):
        pl.semaphore_signal(barrier, inc=1, device_id=z_dev(k), device_id_type=MESH)
        return c

    def greet_y(k, c):
        pl.semaphore_signal(barrier, inc=1, device_id=(lax.rem(d + k, nd), t, a), device_id_type=MESH)
        return c

    def greet_x(k, c):
        pl.semaphore_signal(barrier, inc=1, device_id=x_dev(k), device_id_type=MESH)
        return c
    lax.fori_loop(1, nt, greet_z, 0)
    lax.fori_loop(1, nd, greet_y, 0)
    lax.fori_loop(1, na, greet_x, 0)

    for fetch in fetches[:6]:
        fetch.wait()
    idx_col = column_of(idx_ref[...].astype(F32), rows)
    table = slot_ref.shape[1]
    slot_col = jnp.sum(
        jnp.where(idx_col == iota((rows, table), 1).astype(F32), slot_ref[...].astype(F32), 0.0),
        axis=1, keepdims=True,
    )
    owner_col = jnp.floor(slot_col * (1.0 / holding))
    local_col = slot_col - holding * owner_col
    owner_row = row_of(owner_col, rows)
    earlier = (owner_row == owner_col) & (iota((rows, rows), 1) < iota((rows, rows), 0))
    pos_col = jnp.sum(jnp.where(earlier, 1.0, 0.0), axis=1, keepdims=True)
    lane = iota((rows, lanes), 1)
    tags = jnp.where(lane == 0, owner_col * CAP + pos_col, jnp.where(lane == 1, local_col, 0.0))

    att = attend(q_ref, k_ref, v_ref, len_ref[...].astype(F32), rows, groups, cache)
    swap = regroup(rows, groups)
    att = dot(swap, att).astype(BF16)
    mine = pl.ds(pl.multiple_of(t * rows, rows), rows)
    for g in range(groups):
        xg[mine, g * 128 : (g + 1) * 128] = att[g * rows : (g + 1) * rows, :]
    xg[mine, feat : feat + lanes] = tags.astype(BF16)

    pl.semaphore_wait(barrier, (nt - 1) + (nd - 1) + (na - 1))

    def z_copy(k, block):
        part = xg.at[pl.ds(pl.multiple_of(block * rows, rows), rows)]
        return pltpu.make_async_remote_copy(
            src_ref=part, dst_ref=part, send_sem=z_send.at[k], recv_sem=z_recv.at[k],
            device_id=z_dev(k), device_id_type=MESH)

    def z_start(k, c):
        z_copy(k, t).start()
        return c
    lax.fori_loop(1, nt, z_start, 0)

    fetches[6].wait()
    fetches[7].wait()
    step = 256 // groups
    swap_w = regroup(step, groups)
    for b in range(holding * half // step):
        part = slice(b * step * groups, (b + 1) * step * groups)
        up = dot(swap_w, up_ref[part, :]).astype(BF16)
        for g in range(nt):
            upp[g, b * step : (b + 1) * step, :] = up[g * step : (g + 1) * step, :]
        down = dot(swap_w, down_ref[part, :]).astype(BF16)
        for g in range(groups):
            downp[b * step : (b + 1) * step, g * 128 : (g + 1) * 128] = down[g * step : (g + 1) * step, :]
    upg[t] = upp[t]

    def z_wait(k, c):
        z_copy(k, lax.rem(t - k + nt, nt)).wait_recv()
        return c
    lax.fori_loop(1, nt, z_wait, 0)

    tag = xg[:, feat : feat + lanes].astype(F32)
    codes, local = tag[:, 0:1], tag[:, 1:2]
    owners = jnp.floor(codes * (1.0 / CAP))
    pos = codes - CAP * owners
    owner_d = jnp.floor(owners * (1.0 / nt))
    owner_t = owners - nt * owner_d
    place = (iota((all_rows, 1), 0) // rows).astype(F32) * CAP + pos
    target = owner_d * spots + place
    target_row = row_of(target, all_rows)
    here_row = row_of(jnp.where(owner_t == t.astype(F32), 1.0, 0.0), all_rows)
    route = jnp.where(iota((slots, all_rows), 0).astype(F32) == target_row, 1.0, 0.0)
    wide_lane = iota((all_rows, lanes), 1)
    places = jnp.where((wide_lane - 8).astype(F32) == owner_t, local + 1.0, 0.0).astype(BF16)
    beside = dot(route.astype(BF16), places)
    route = (route * here_row).astype(BF16)
    beside = beside + jnp.where(iota((slots, lanes), 1) == 1, dot(route, xg[:, feat : feat + lanes]), 0.0)
    pk[:, :feat] = dot(route, xg[:, :feat]).astype(BF16)
    pk[:, feat : feat + lanes] = beside.astype(BF16)

    def y_copy(m):
        return pltpu.make_async_remote_copy(
            src_ref=pk.at[pl.ds(pl.multiple_of(dp_at(m) * spots, spots), spots)],
            dst_ref=rx.at[pl.ds(back(m) * spots, spots)], send_sem=y_send.at[m],
            recv_sem=y_recv.at[back(m)], device_id=(dp_at(m), t, a), device_id_type=MESH)

    def y_arrival(m):
        return pltpu.make_async_remote_copy(
            src_ref=pk.at[pl.ds(pl.multiple_of(dp_at(m) * spots, spots), spots)],
            dst_ref=rx.at[pl.ds(m * spots, spots)], send_sem=y_send.at[m],
            recv_sem=y_recv.at[m], device_id=(dp_at(m), t, a), device_id_type=MESH)

    for m in range(1, nd):
        y_copy(m).start()
    rx[0:spots, :] = pk[pl.ds(pl.multiple_of(d * spots, spots), spots), :]

    def u_copy(k):
        return pltpu.make_async_remote_copy(
            src_ref=upp.at[lax.rem(t + k, nt)], dst_ref=upg.at[t], send_sem=u_send.at[k],
            recv_sem=u_recv.at[k], device_id=z_dev(k), device_id_type=MESH)

    def u_start(k, c):
        u_copy(k).start()
        return c
    lax.fori_loop(1, nt, u_start, 0)

    def f_copy(m):
        return pltpu.make_async_remote_copy(
            src_ref=ret_tx.at[m], dst_ref=ret_rx.at[back(m)], send_sem=f_send.at[m],
            recv_sem=f_recv.at[back(m)], device_id=(dp_at(m), t, a), device_id_type=MESH)

    def f_arrival(m):
        return pltpu.make_async_remote_copy(
            src_ref=ret_tx.at[m], dst_ref=ret_rx.at[m], send_sem=f_send.at[m],
            recv_sem=f_recv.at[m], device_id=(dp_at(m), t, a), device_id_type=MESH)

    def swapped(v):
        return jnp.concatenate([v[:, half:], v[:, :half]], axis=1)

    def packed(run):
        lo, hi = run
        return pl.ds(lo * spots // 2, (hi - lo) * spots // 2)

    def p_copy(c, k):
        return pltpu.make_async_remote_copy(
            src_ref=ptx.at[packed(runs[c])], dst_ref=prx.at[k, packed(runs[c])], send_sem=p_send.at[c, k],
            recv_sem=p_recv.at[c, k], device_id=x_dev(k), device_id_type=MESH)

    def r_copy(c, k, block):
        part = redg.at[block, packed(runs[c])]
        return pltpu.make_async_remote_copy(
            src_ref=part, dst_ref=part, send_sem=r_send.at[c, k],
            recv_sem=r_recv.at[c, k], device_id=z_dev(k), device_id_type=MESH)

    for c, (lo, hi) in enumerate(runs):
        n = (hi - lo) * spots
        part = slice(lo * spots, hi * spots)
        for m in range(max(lo, 1), hi):
            y_arrival(m).wait_recv()
        shrunk = dot_t(rx[part, :feat], downp[...])
        at = iota((n, lanes), 1)
        shrunk = jnp.where((at // half).astype(F32) == rx[part, feat + 1 : feat + 2].astype(F32), shrunk, 0.0)
        shrunk = shrunk + swapped(shrunk)
        shrunk = jnp.where(at[: n // 2] < half, shrunk[: n // 2], shrunk[n // 2 :])
        ptx[packed((lo, hi)), :] = shrunk.astype(BF16)
        for k in range(1, na):
            p_copy(c, k).start()
        for k in range(1, na):
            p_copy(c, k).wait_recv()
            shrunk = shrunk + prx[k, packed((lo, hi)), :].astype(F32)
        redg[t, packed((lo, hi)), :] = shrunk.astype(BF16)

        def r_start(k, s, c=c):
            r_copy(c, k, t).start()
            return s
        lax.fori_loop(1, nt, r_start, 0)

        def r_wait(k, s, c=c):
            r_copy(c, k, lax.rem(t - k + nt, nt)).wait_recv()
            if c == 0:
                u_copy(k).wait_recv()
            return s
        lax.fori_loop(1, nt, r_wait, 0)
        for g in range(nt):
            both = redg[g, packed((lo, hi)), :].astype(F32)
            turned = swapped(both)
            low = at[: n // 2] < half
            spread = jnp.concatenate([jnp.where(low, both, turned), jnp.where(low, turned, both)], axis=0)
            held = rx[part, feat + 8 + g : feat + 9 + g].astype(F32) - 1.0
            spread = jnp.where((at // half).astype(F32) == held, spread, 0.0).astype(BF16)
            grown = dot(spread, upg[g]).astype(BF16)
            ret_tx[lo:hi, g, :, :] = grown.reshape(hi - lo, spots, cols)
        for m in range(max(lo, 1), hi):
            f_copy(m).start()
    ret_rx[0] = ret_tx[0]

    fetches[8].wait()
    x = xg[:, :feat]

    def b_copy(k):
        return pltpu.make_async_remote_copy(
            src_ref=btx.at[k], dst_ref=brx.at[k], send_sem=b_send.at[k],
            recv_sem=b_recv.at[k], device_id=x_dev(k), device_id_type=MESH)
    for k in range(1, na):
        part = pl.ds(pl.multiple_of(lax.rem(a + k, na) * cols, cols), cols)
        btx[k] = dot(x, w_ref[:, part]).astype(BF16)
        b_copy(k).start()
    acc[...] = dot(x, w_ref[:, pl.ds(pl.multiple_of(a * cols, cols), cols)])
    for k in range(1, na):
        b_copy(k).wait_recv()
        acc[...] += brx[k].astype(F32)

    target = owners * spots + place
    total = acc[...]
    span = nt * spots
    for m in range(nd):
        if m:
            f_arrival(m).wait_recv()
        place_of = (iota((all_rows, span), 1) + dp_at(m) * span).astype(F32)
        pick = jnp.where(place_of == target, 1.0, 0.0).astype(BF16)
        total = total + dot(pick, ret_rx[m].reshape(span, cols))
    out_ref[...] = total.astype(BF16)

    def drain_z(k, c):
        z_copy(k, t).wait_send()
        u_copy(k).wait_send()
        for r in range(len(runs)):
            r_copy(r, k, t).wait_send()
        return c
    lax.fori_loop(1, nt, drain_z, 0)
    for m in range(1, nd):
        y_copy(m).wait_send()
        f_copy(m).wait_send()
    for k in range(1, na):
        b_copy(k).wait_send()
        for c in range(len(runs)):
            p_copy(c, k).wait_send()


def body(sizes, q, kc, vc, lengths, index, table, w, down, up):
    nd, nt, na = sizes
    rows, groups, _, width = q.shape
    cache = kc.shape[1]
    holding, rank = down.shape[0], down.shape[1]
    feat = groups * width
    columns = w.shape[-1]
    cols = columns // na
    spots = nt * CAP
    slots = nd * spots
    wide = feat + holding * rank
    hr = holding * rank
    parts = len(order_of(nd // 2)[1])
    dma = pltpu.SemaphoreType.DMA
    return pl.pallas_call(
        functools.partial(kernel, nd, nt, na, groups, cache, holding),
        out_shape=jax.ShapeDtypeStruct((nt * rows, cols), BF16),
        in_specs=[pl.BlockSpec(memory_space=pltpu.HBM)] * 9,
        out_specs=pl.BlockSpec(memory_space=pltpu.VMEM),
        scratch_shapes=[
            pltpu.VMEM((rows * groups, width), BF16),
            pltpu.VMEM((rows * cache, width), BF16),
            pltpu.VMEM((rows * cache, width), BF16),
            pltpu.VMEM((1, rows), jnp.int32),
            pltpu.VMEM((1, rows), jnp.int32),
            pltpu.VMEM((1, table.shape[0]), jnp.int32),
            pltpu.VMEM((hr * groups, width), BF16),
            pltpu.VMEM((hr * nt, cols), BF16),
            pltpu.VMEM((nt * rows, wide), BF16),
            pltpu.VMEM((slots, wide), BF16),
            pltpu.VMEM((slots, wide), BF16),
            pltpu.VMEM((feat, columns), BF16),
            pltpu.VMEM((hr, feat), BF16),
            pltpu.VMEM((nt, hr, cols), BF16),
            pltpu.VMEM((nt, hr, cols), BF16),
            pltpu.VMEM((na, nt * rows, cols), BF16),
            pltpu.VMEM((na, nt * rows, cols), BF16),
            pltpu.VMEM((nt * rows, cols), F32),
            pltpu.VMEM((slots // 2, hr), BF16),
            pltpu.VMEM((na, slots // 2, hr), BF16),
            pltpu.VMEM((nt, slots // 2, hr), BF16),
            pltpu.VMEM((nd, nt, spots, cols), BF16),
            pltpu.VMEM((nd, nt, spots, cols), BF16),
            dma((9,)),
            dma((nt,)), dma((nt,)), dma((nt,)), dma((nt,)),
            dma((nd,)), dma((nd,)),
            dma((na,)), dma((na,)), dma((parts, na)), dma((parts, na)),
            dma((parts, nt)), dma((parts, nt)),
            dma((nd,)), dma((nd,)),
        ],
        compiler_params=pltpu.CompilerParams(
            collective_id=0, has_side_effects=True, vmem_limit_bytes=60 * 1024 * 1024
        ),
    )(
        q.reshape(rows * groups, width),
        kc.reshape(rows * cache, width),
        vc.reshape(rows * cache, width),
        lengths.reshape(1, rows),
        index.reshape(1, rows),
        table.reshape(1, -1),
        w.reshape(feat, columns),
        down.reshape(hr * groups, width),
        up.reshape(hr * nt, cols),
    )


def solution(mesh):
    sizes = tuple(mesh.shape[name] for name in ("dp", "tensor", "adapter"))
    return jax.shard_map(
        functools.partial(body, sizes),
        mesh=mesh,
        in_specs=(
            P(("dp", "tensor"), None, "adapter", None),
            P(("dp", "tensor"), None, "adapter", None),
            P(("dp", "tensor"), None, "adapter", None),
            P(("dp", "tensor")),
            P(("dp", "tensor")),
            P(),
            P(None, "adapter", None, "tensor"),
            P(("dp", "tensor"), None, None, "adapter", None),
            P(("dp", "tensor"), None, None, "adapter"),
        ),
        out_specs=P("dp", ("tensor", "adapter")),
        check_vma=False,
    )
```

time: 102 us -> 84.8 us (0.83); the launches traced: 100 us -> 84.7 us
  Pallas kernels: 91.2 us -> 83.1 us
  local copies, waits for them, and re-layouts: 8.87 us -> 1.57 us
    pallas_call x1, Pallas kernels: 91.2 us -> 83.1 us  [body(): pl.pallas_call(functools.partial(kernel, nd, nt, na, groups, cache, holdi...]
    unnamed x19 -> x1, local copies, waits for them, and re-layouts: 8.87 us -> 1.57 us
where the time goes in v2:
time: 84.8 us; the launch traced here: 84.7 us
  Pallas kernels  83.1 us (98%)
  local copies, waits for them, and re-layouts  1.57 us (2%)
    pallas_call x1, Pallas kernels, body(): pl.pallas_call(functools.partial(kernel, nd, nt, na, groups, cache, holdi...  83.1 us

profile of v2, /device:TPU:1, one launch (start us, length us, event | category | flops | bytes accessed | tf_op | source)
XLA Modules:
  0.0 84.7 jit_solution(3242768099351550216)
XLA Ops:
  0.0 83.1 %shard_map.91 = bf16[256,256]{1,0:T(8,128)(2,1)} custom-call(bf16[256,128]{1,0:T(8,128)(2,1)} %bitcast.14, bf16[512,128]{1,0:T(8,128)(2,1)} %bitcast.12, bf16[512,128]{1,0:T(8,128)(2,1)} %bitcast.13, s32[1,32]{1,0:T(1,128)} %bitcast.16, s32[1,32]{1,0:T(1,128)} %bitcast.17, s32[1,256]{1,0:T(1,128)} %bitcast.15, bf16[1024,1024]{1,0:T(8,128)(2,1)} %bitcast.9, ...), custom_call_target="tpu_custom_call" | custom-call | tf_op jit(solution)/shard_map/pallas_call | solution.py:362
  83.1 1.6 %copy.11 = bf16[256,256]{1,0:T(8,128)(2,1)} copy(bf16[256,256]{1,0:T(8,128)(2,1)} %shard_map.91) | data formatting | bytes 262144

commit v3 on v2

--- a/solution.py
+++ b/solution.py
@@ -66,11 +66,13 @@
 
 
 def order_of(chips):
-    near = [0]
-    for j in range(1, chips // 2 + 1):
-        near += [j] if 2 * j == chips else [j, chips - j]
-    cuts = sorted({0, min(3, chips), min(5, chips), chips})
-    return near, [(2 * lo, 2 * hi) for lo, hi in zip(cuts[:-1], cuts[1:])]
+    far = chips // 2
+    near = [0, 1, -1, 2, -2] + list(range(3, far + 1)) + [-j for j in range(3, far)]
+    return near, [(0, 6), (6, 10), (10, 2 * chips)]
+
+
+def sign(j):
+    return (j > 0) - (j < 0)
 
 
 def kernel(
@@ -79,7 +81,7 @@
     q_ref, k_ref, v_ref, len_ref, idx_ref, slot_ref, down_ref, up_ref,
     xg, pk, rx, w_ref, downp, upp, upg, btx, brx, acc, ptx, prx, redg, ret_tx, ret_rx,
     in_sem, z_send, z_recv, u_send, u_recv, y_send, y_recv, b_send, b_recv, p_send, p_recv,
-    r_send, r_recv, f_send, f_recv,
+    r_send, r_recv, f_send, f_recv, d_send, d_recv, v_send, v_recv,
 ):
     d, t, a = lax.axis_index("dp"), lax.axis_index("tensor"), lax.axis_index("adapter")
     rows = q_ref.shape[0] // groups
@@ -94,11 +96,27 @@
     near, runs = order_of(chips)
     chip, core = d // 2, d % 2
 
-    def dp_at(m):
-        return 2 * lax.rem(chip + near[m // 2], chips) + lax.rem(core + m % 2, 2)
-
-    def back(m):
-        return 2 * near.index((chips - near[m // 2]) % chips) + m % 2
+    def at_chip(j, m):
+        return 2 * lax.rem(chip + j + chips, chips) + lax.rem(core + m % 2, 2)
+
+    def owner_at(m):
+        return at_chip(near[m // 2], m)
+
+    def server_at(m):
+        return at_chip(near[m // 2] - sign(near[m // 2]), m)
+
+    def served_at(m):
+        return at_chip(sign(near[m // 2]) - near[m // 2], m)
+
+    def maps_of(lo, hi):
+        found = []
+        for m in range(lo, hi):
+            side = (0, 1, 2)[sign(near[m // 2])]
+            if found and found[-1][2] == side:
+                found[-1][1] = m + 1
+            else:
+                found.append([m, m + 1, side])
+        return found
 
     def z_dev(k):
         return (d, lax.rem(t + k, nt), a)
@@ -109,8 +127,8 @@
     fetches = [
         pltpu.make_async_copy(src, dst, in_sem.at[n])
         for n, (src, dst) in enumerate((
-            (idx_hbm, idx_ref), (slot_hbm, slot_ref), (len_hbm, len_ref), (q_hbm, q_ref), (k_hbm, k_ref),
-            (v_hbm, v_ref), (up_hbm, up_ref), (down_hbm, down_ref), (w_hbm, w_ref)))
+            (up_hbm, up_ref), (down_hbm, down_ref), (idx_hbm, idx_ref), (slot_hbm, slot_ref), (len_hbm, len_ref),
+            (q_hbm, q_ref), (k_hbm, k_ref), (v_hbm, v_ref), (w_hbm, w_ref)))
     ]
     for fetch in fetches:
         fetch.start()
@@ -131,7 +149,51 @@
     lax.fori_loop(1, nd, greet_y, 0)
     lax.fori_loop(1, na, greet_x, 0)
 
-    for fetch in fetches[:6]:
+    fetches[0].wait()
+    fetches[1].wait()
+    step = 256 // groups
+    swap_w = regroup(step, groups)
+    for b in range(holding * half // step):
+        part = slice(b * step * groups, (b + 1) * step * groups)
+        up = dot(swap_w, up_ref[part, :]).astype(BF16)
+        for g in range(nt):
+            upp[g, b * step : (b + 1) * step, :] = up[g * step : (g + 1) * step, :]
+        down = dot(swap_w, down_ref[part, :]).astype(BF16)
+        for g in range(groups):
+            downp[0, b * step : (b + 1) * step, g * 128 : (g + 1) * 128] = down[g * step : (g + 1) * step, :]
+    upg[0, t] = upp[t]
+
+    pl.semaphore_wait(barrier, (nt - 1) + (nd - 1) + (na - 1))
+
+    def u_copy(k):
+        return pltpu.make_async_remote_copy(
+            src_ref=upp.at[lax.rem(t + k, nt)], dst_ref=upg.at[0, t], send_sem=u_send.at[k],
+            recv_sem=u_recv.at[k], device_id=z_dev(k), device_id_type=MESH)
+
+    def u_arrival(k):
+        return pltpu.make_async_remote_copy(
+            src_ref=upp.at[lax.rem(t + k, nt)], dst_ref=upg.at[0, lax.rem(t - k + nt, nt)], send_sem=u_send.at[k],
+            recv_sem=u_recv.at[k], device_id=z_dev(k), device_id_type=MESH)
+
+    def beside_dev(side):
+        return (at_chip(1 if side == 1 else -1, 0), t, a)
+
+    def d_copy(side):
+        return pltpu.make_async_remote_copy(
+            src_ref=downp.at[0], dst_ref=downp.at[3 - side], send_sem=d_send.at[side],
+            recv_sem=d_recv.at[3 - side], device_id=beside_dev(side), device_id_type=MESH)
+
+    def v_copy(side, k):
+        block = lax.rem(t - k + nt, nt)
+        return pltpu.make_async_remote_copy(
+            src_ref=upg.at[0, block], dst_ref=upg.at[3 - side, block], send_sem=v_send.at[side, k],
+            recv_sem=v_recv.at[3 - side, k], device_id=beside_dev(side), device_id_type=MESH)
+
+    for side in (1, 2):
+        d_copy(side).start()
+        v_copy(side, 0).start()
+
+    for fetch in fetches[2:8]:
         fetch.wait()
     idx_col = column_of(idx_ref[...].astype(F32), rows)
     table = slot_ref.shape[1]
@@ -155,37 +217,33 @@
         xg[mine, g * 128 : (g + 1) * 128] = att[g * rows : (g + 1) * rows, :]
     xg[mine, feat : feat + lanes] = tags.astype(BF16)
 
-    pl.semaphore_wait(barrier, (nt - 1) + (nd - 1) + (na - 1))
-
-    def z_copy(k, block):
+    def z_copy(k, hop):
+        block = lax.rem(t - k + nt, nt)
+        part = xg.at[pl.ds(pl.multiple_of(block * rows, rows), rows)]
+        far = (k + hop) % nt
+        return pltpu.make_async_remote_copy(
+            src_ref=part, dst_ref=part, send_sem=z_send.at[far], recv_sem=z_recv.at[far],
+            device_id=z_dev(hop % nt), device_id_type=MESH)
+
+    def z_arrival(k):
+        block = lax.rem(t - k + nt, nt)
         part = xg.at[pl.ds(pl.multiple_of(block * rows, rows), rows)]
         return pltpu.make_async_remote_copy(
             src_ref=part, dst_ref=part, send_sem=z_send.at[k], recv_sem=z_recv.at[k],
             device_id=z_dev(k), device_id_type=MESH)
 
-    def z_start(k, c):
-        z_copy(k, t).start()
-        return c
-    lax.fori_loop(1, nt, z_start, 0)
-
-    fetches[6].wait()
-    fetches[7].wait()
-    step = 256 // groups
-    swap_w = regroup(step, groups)
-    for b in range(holding * half // step):
-        part = slice(b * step * groups, (b + 1) * step * groups)
-        up = dot(swap_w, up_ref[part, :]).astype(BF16)
-        for g in range(nt):
-            upp[g, b * step : (b + 1) * step, :] = up[g * step : (g + 1) * step, :]
-        down = dot(swap_w, down_ref[part, :]).astype(BF16)
-        for g in range(groups):
-            downp[b * step : (b + 1) * step, g * 128 : (g + 1) * 128] = down[g * step : (g + 1) * step, :]
-    upg[t] = upp[t]
-
-    def z_wait(k, c):
-        z_copy(k, lax.rem(t - k + nt, nt)).wait_recv()
-        return c
-    lax.fori_loop(1, nt, z_wait, 0)
+    z_first = [(0, 2), (0, -2), (0, 1), (0, -1)]
+    z_second = {2: [(2, 2), (2, 1)], nt - 2: [(nt - 2, -1)]}
+    for k, hop in z_first:
+        z_copy(k, hop).start()
+    for k, copies in z_second.items():
+        z_arrival(k).wait_recv()
+        for block, hop in copies:
+            z_copy(block, hop).start()
+
+    for k in range(1, nt):
+        if k not in z_second:
+            z_arrival(k).wait_recv()
 
     tag = xg[:, feat : feat + lanes].astype(F32)
     codes, local = tag[:, 0:1], tag[:, 1:2]
@@ -208,39 +266,36 @@
 
     def y_copy(m):
         return pltpu.make_async_remote_copy(
-            src_ref=pk.at[pl.ds(pl.multiple_of(dp_at(m) * spots, spots), spots)],
-            dst_ref=rx.at[pl.ds(back(m) * spots, spots)], send_sem=y_send.at[m],
-            recv_sem=y_recv.at[back(m)], device_id=(dp_at(m), t, a), device_id_type=MESH)
-
-    def y_arrival(m):
-        return pltpu.make_async_remote_copy(
-            src_ref=pk.at[pl.ds(pl.multiple_of(dp_at(m) * spots, spots), spots)],
+            src_ref=pk.at[pl.ds(pl.multiple_of(owner_at(m) * spots, spots), spots)],
             dst_ref=rx.at[pl.ds(m * spots, spots)], send_sem=y_send.at[m],
-            recv_sem=y_recv.at[m], device_id=(dp_at(m), t, a), device_id_type=MESH)
-
-    for m in range(1, nd):
+            recv_sem=y_recv.at[m], device_id=(server_at(m), t, a), device_id_type=MESH)
+
+    own = [m for m in range(nd) if m % 2 == 0 and abs(near[m // 2]) < 2]
+    others = [m for m in range(nd) if m not in own]
+    for m in others:
         y_copy(m).start()
-    rx[0:spots, :] = pk[pl.ds(pl.multiple_of(d * spots, spots), spots), :]
-
-    def u_copy(k):
-        return pltpu.make_async_remote_copy(
-            src_ref=upp.at[lax.rem(t + k, nt)], dst_ref=upg.at[t], send_sem=u_send.at[k],
-            recv_sem=u_recv.at[k], device_id=z_dev(k), device_id_type=MESH)
-
-    def u_start(k, c):
+    near_z = sorted(range(1, nt), key=lambda k: min(k, nt - k))
+    for k in near_z:
         u_copy(k).start()
-        return c
-    lax.fori_loop(1, nt, u_start, 0)
+
+    def hand_on(first, last):
+        for k in near_z[first:last]:
+            u_arrival(k).wait_recv()
+            for side in (1, 2):
+                v_copy(side, k).start()
+
+    fetches[8].wait()
+    x = xg[:, :feat]
+    for k in range(1, na):
+        part = pl.ds(pl.multiple_of(lax.rem(a + k, na) * cols, cols), cols)
+        btx[k] = dot(x, w_ref[:, part]).astype(BF16)
+    for m in own:
+        rx[m * spots : (m + 1) * spots, :] = pk[pl.ds(pl.multiple_of(owner_at(m) * spots, spots), spots), :]
 
     def f_copy(m):
         return pltpu.make_async_remote_copy(
-            src_ref=ret_tx.at[m], dst_ref=ret_rx.at[back(m)], send_sem=f_send.at[m],
-            recv_sem=f_recv.at[back(m)], device_id=(dp_at(m), t, a), device_id_type=MESH)
-
-    def f_arrival(m):
-        return pltpu.make_async_remote_copy(
             src_ref=ret_tx.at[m], dst_ref=ret_rx.at[m], send_sem=f_send.at[m],
-            recv_sem=f_recv.at[m], device_id=(dp_at(m), t, a), device_id_type=MESH)
+            recv_sem=f_recv.at[m], device_id=(served_at(m), t, a), device_id_type=MESH)
 
     def swapped(v):
         return jnp.concatenate([v[:, half:], v[:, :half]], axis=1)
@@ -260,59 +315,89 @@
             src_ref=part, dst_ref=part, send_sem=r_send.at[c, k],
             recv_sem=r_recv.at[c, k], device_id=z_dev(k), device_id_type=MESH)
 
-    for c, (lo, hi) in enumerate(runs):
+    def down_of(c):
+        lo, hi = runs[c]
         n = (hi - lo) * spots
-        part = slice(lo * spots, hi * spots)
-        for m in range(max(lo, 1), hi):
-            y_arrival(m).wait_recv()
-        shrunk = dot_t(rx[part, :feat], downp[...])
+        for m in range(lo, hi):
+            if m in others:
+                y_copy(m).wait_recv()
+        if c == 0:
+            for side in (1, 2):
+                d_copy(side).wait_recv()
+        shrunk = jnp.concatenate(
+            [dot_t(rx[first * spots : last * spots, :feat], downp[side]) for first, last, side in maps_of(lo, hi)], axis=0)
         at = iota((n, lanes), 1)
-        shrunk = jnp.where((at // half).astype(F32) == rx[part, feat + 1 : feat + 2].astype(F32), shrunk, 0.0)
+        held = rx[lo * spots : hi * spots, feat + 1 : feat + 2].astype(F32)
+        shrunk = jnp.where((at // half).astype(F32) == held, shrunk, 0.0)
         shrunk = shrunk + swapped(shrunk)
         shrunk = jnp.where(at[: n // 2] < half, shrunk[: n // 2], shrunk[n // 2 :])
-        ptx[packed((lo, hi)), :] = shrunk.astype(BF16)
+        ptx[packed(runs[c]), :] = shrunk.astype(BF16)
         for k in range(1, na):
             p_copy(c, k).start()
+        return shrunk
+
+    def sum_of(c, shrunk):
         for k in range(1, na):
             p_copy(c, k).wait_recv()
-            shrunk = shrunk + prx[k, packed((lo, hi)), :].astype(F32)
-        redg[t, packed((lo, hi)), :] = shrunk.astype(BF16)
-
-        def r_start(k, s, c=c):
+            shrunk = shrunk + prx[k, packed(runs[c]), :].astype(F32)
+        redg[t, packed(runs[c]), :] = shrunk.astype(BF16)
+
+        def r_start(k, s):
             r_copy(c, k, t).start()
             return s
         lax.fori_loop(1, nt, r_start, 0)
 
-        def r_wait(k, s, c=c):
+    def up_of(c):
+        lo, hi = runs[c]
+        n = (hi - lo) * spots
+
+        def r_wait(k, s):
             r_copy(c, k, lax.rem(t - k + nt, nt)).wait_recv()
-            if c == 0:
-                u_copy(k).wait_recv()
             return s
         lax.fori_loop(1, nt, r_wait, 0)
+        if c == 0:
+            def v_wait(k, s):
+                for side in (1, 2):
+                    v_copy(side, k).wait_recv()
+                return s
+            lax.fori_loop(0, nt, v_wait, 0)
+        at = iota((n, lanes), 1)
+        low = at[: n // 2] < half
         for g in range(nt):
-            both = redg[g, packed((lo, hi)), :].astype(F32)
+            both = redg[g, packed(runs[c]), :].astype(F32)
             turned = swapped(both)
-            low = at[: n // 2] < half
             spread = jnp.concatenate([jnp.where(low, both, turned), jnp.where(low, turned, both)], axis=0)
-            held = rx[part, feat + 8 + g : feat + 9 + g].astype(F32) - 1.0
+            held = rx[lo * spots : hi * spots, feat + 8 + g : feat + 9 + g].astype(F32) - 1.0
             spread = jnp.where((at // half).astype(F32) == held, spread, 0.0).astype(BF16)
-            grown = dot(spread, upg[g]).astype(BF16)
-            ret_tx[lo:hi, g, :, :] = grown.reshape(hi - lo, spots, cols)
-        for m in range(max(lo, 1), hi):
-            f_copy(m).start()
-    ret_rx[0] = ret_tx[0]
-
-    fetches[8].wait()
-    x = xg[:, :feat]
+            for first, last, side in maps_of(lo, hi):
+                grown = dot(spread[(first - lo) * spots : (last - lo) * spots], upg[side, g]).astype(BF16)
+                ret_tx[first:last, g, :, :] = grown.reshape(last - first, spots, cols)
+        for m in range(lo, hi):
+            if m in others:
+                f_copy(m).start()
 
     def b_copy(k):
         return pltpu.make_async_remote_copy(
             src_ref=btx.at[k], dst_ref=brx.at[k], send_sem=b_send.at[k],
             recv_sem=b_recv.at[k], device_id=x_dev(k), device_id_type=MESH)
+
+    s0 = down_of(0)
+    sum_of(0, s0)
+    hand_on(0, 2)
+    s1 = down_of(1)
+    hand_on(2, 4)
+    sum_of(1, s1)
+    s2 = down_of(2)
+    hand_on(4, 6)
+    sum_of(2, s2)
+    hand_on(6, nt)
     for k in range(1, na):
-        part = pl.ds(pl.multiple_of(lax.rem(a + k, na) * cols, cols), cols)
-        btx[k] = dot(x, w_ref[:, part]).astype(BF16)
         b_copy(k).start()
+    up_of(0)
+    up_of(1)
+    up_of(2)
+    for m in own:
+        ret_rx[m] = ret_tx[m]
     acc[...] = dot(x, w_ref[:, pl.ds(pl.multiple_of(a * cols, cols), cols)])
     for k in range(1, na):
         b_copy(k).wait_recv()
@@ -322,21 +407,30 @@
     total = acc[...]
     span = nt * spots
     for m in range(nd):
-        if m:
-            f_arrival(m).wait_recv()
-        place_of = (iota((all_rows, span), 1) + dp_at(m) * span).astype(F32)
+        if m in others:
+            f_copy(m).wait_recv()
+        place_of = (iota((all_rows, span), 1) + owner_at(m) * span).astype(F32)
         pick = jnp.where(place_of == target, 1.0, 0.0).astype(BF16)
         total = total + dot(pick, ret_rx[m].reshape(span, cols))
     out_ref[...] = total.astype(BF16)
 
     def drain_z(k, c):
-        z_copy(k, t).wait_send()
         u_copy(k).wait_send()
         for r in range(len(runs)):
             r_copy(r, k, t).wait_send()
         return c
     lax.fori_loop(1, nt, drain_z, 0)
-    for m in range(1, nd):
+    for k, hop in z_first + [copy for copies in z_second.values() for copy in copies]:
+        z_copy(k, hop).wait_send()
+
+    def drain_v(k, c):
+        for side in (1, 2):
+            v_copy(side, k).wait_send()
+        return c
+    lax.fori_loop(0, nt, drain_v, 0)
+    for side in (1, 2):
+        d_copy(side).wait_send()
+    for m in others:
         y_copy(m).wait_send()
         f_copy(m).wait_send()
     for k in range(1, na):
@@ -377,9 +471,9 @@
             pltpu.VMEM((slots, wide), BF16),
             pltpu.VMEM((slots, wide), BF16),
             pltpu.VMEM((feat, columns), BF16),
-            pltpu.VMEM((hr, feat), BF16),
+            pltpu.VMEM((3, hr, feat), BF16),
             pltpu.VMEM((nt, hr, cols), BF16),
-            pltpu.VMEM((nt, hr, cols), BF16),
+            pltpu.VMEM((3, nt, hr, cols), BF16),
             pltpu.VMEM((na, nt * rows, cols), BF16),
             pltpu.VMEM((na, nt * rows, cols), BF16),
             pltpu.VMEM((nt * rows, cols), F32),
@@ -394,6 +488,7 @@
             dma((na,)), dma((na,)), dma((parts, na)), dma((parts, na)),
             dma((parts, nt)), dma((parts, nt)),
             dma((nd,)), dma((nd,)),
+            dma((3,)), dma((3,)), dma((3, nt)), dma((3, nt)),
         ],
         compiler_params=pltpu.CompilerParams(
             collective_id=0, has_side_effects=True, vmem_limit_bytes=60 * 1024 * 1024

time: 84.8 us -> 75.2 us (0.89)
  the two profiles are of different devices: /device:TPU:1 before, /device:TPU:9 now
where the time goes in v3:
time: 75.2 us; the launch traced here: 75.1 us
  Pallas kernels  73.5 us (98%)
  local copies, waits for them, and re-layouts  1.57 us (2%)
    pallas_call x1, Pallas kernels, body(): pl.pallas_call(functools.partial(kernel, nd, nt, na, groups, cache, holdi...  73.5 us
    unnamed x1, local copies, waits for them, and re-layouts  1.57 us

profile of v3, /device:TPU:9, one launch (start us, length us, event | category | flops | bytes accessed | tf_op | source)
XLA Modules:
  0.0 75.1 jit_solution(8210547092332302565)
XLA Ops:
  0.0 73.5 %shard_map.91 = bf16[256,256]{1,0:T(8,128)(2,1)} custom-call(bf16[256,128]{1,0:T(8,128)(2,1)} %bitcast.14, bf16[512,128]{1,0:T(8,128)(2,1)} %bitcast.12, bf16[512,128]{1,0:T(8,128)(2,1)} %bitcast.13, s32[1,32]{1,0:T(1,128)} %bitcast.16, s32[1,32]{1,0:T(1,128)} %bitcast.17, s32[1,256]{1,0:T(1,128)} %bitcast.15, bf16[1024,1024]{1,0:T(8,128)(2,1)} %bitcast.9, ...), custom_call_target="tpu_custom_call" | custom-call | tf_op jit(solution)/shard_map/pallas_call | solution.py:456
  73.5 1.6 %copy.11 = bf16[256,256]{1,0:T(8,128)(2,1)} copy(bf16[256,256]{1,0:T(8,128)(2,1)} %shard_map.91) | data formatting | bytes 262144

commit v4 on v3

--- a/solution.py
+++ b/solution.py
@@ -66,9 +66,13 @@
 
 
 def order_of(chips):
-    far = chips // 2
-    near = [0, 1, -1, 2, -2] + list(range(3, far + 1)) + [-j for j in range(3, far)]
+    half = chips // 2
+    near = [0, 1, -1, 2, -2] + list(range(3, half + 1)) + [-j for j in range(3, half)]
     return near, [(0, 6), (6, 10), (10, 2 * chips)]
+
+
+def ring_order(n):
+    return sorted(range(n), key=lambda k: min(k, n - k))
 
 
 def sign(j):
@@ -79,9 +83,9 @@
     nd, nt, na, groups, cache, holding,
     q_hbm, k_hbm, v_hbm, len_hbm, idx_hbm, slot_hbm, w_hbm, down_hbm, up_hbm, out_ref,
     q_ref, k_ref, v_ref, len_ref, idx_ref, slot_ref, down_ref, up_ref,
-    xg, pk, rx, w_ref, downp, upp, upg, btx, brx, acc, ptx, prx, redg, ret_tx, ret_rx,
+    xg, tg, pk, rx, w_ref, downp, upp, upg, btx, brx, acc, ptx, prx, redg, ret_tx, ret_rx,
     in_sem, z_send, z_recv, u_send, u_recv, y_send, y_recv, b_send, b_recv, p_send, p_recv,
-    r_send, r_recv, f_send, f_recv, d_send, d_recv, v_send, v_recv,
+    r_send, r_recv, f_send, f_recv, d_send, d_recv, v_send, v_recv, t_send, t_recv,
 ):
     d, t, a = lax.axis_index("dp"), lax.axis_index("tensor"), lax.axis_index("adapter")
     rows = q_ref.shape[0] // groups
@@ -96,22 +100,26 @@
     near, runs = order_of(chips)
     chip, core = d // 2, d % 2
 
+    def away(m):
+        j = near[m // 2]
+        return -j if 2 * j == chips and m % 2 else j
+
     def at_chip(j, m):
         return 2 * lax.rem(chip + j + chips, chips) + lax.rem(core + m % 2, 2)
 
     def owner_at(m):
-        return at_chip(near[m // 2], m)
+        return at_chip(away(m), m)
 
     def server_at(m):
-        return at_chip(near[m // 2] - sign(near[m // 2]), m)
+        return at_chip(away(m) - sign(away(m)), m)
 
     def served_at(m):
-        return at_chip(sign(near[m // 2]) - near[m // 2], m)
+        return at_chip(sign(away(m)) - away(m), m)
 
     def maps_of(lo, hi):
         found = []
         for m in range(lo, hi):
-            side = (0, 1, 2)[sign(near[m // 2])]
+            side = (0, 1, 2)[sign(away(m))]
             if found and found[-1][2] == side:
                 found[-1][1] = m + 1
             else:
@@ -127,8 +135,8 @@
     fetches = [
         pltpu.make_async_copy(src, dst, in_sem.at[n])
         for n, (src, dst) in enumerate((
-            (up_hbm, up_ref), (down_hbm, down_ref), (idx_hbm, idx_ref), (slot_hbm, slot_ref), (len_hbm, len_ref),
-            (q_hbm, q_ref), (k_hbm, k_ref), (v_hbm, v_ref), (w_hbm, w_ref)))
+            (q_hbm, q_ref), (k_hbm, k_ref), (len_hbm, len_ref), (v_hbm, v_ref), (idx_hbm, idx_ref),
+            (slot_hbm, slot_ref), (up_hbm, up_ref), (down_hbm, down_ref), (w_hbm, w_ref)))
     ]
     for fetch in fetches:
         fetch.start()
@@ -149,51 +157,40 @@
     lax.fori_loop(1, nd, greet_y, 0)
     lax.fori_loop(1, na, greet_x, 0)
 
-    fetches[0].wait()
-    fetches[1].wait()
-    step = 256 // groups
-    swap_w = regroup(step, groups)
-    for b in range(holding * half // step):
-        part = slice(b * step * groups, (b + 1) * step * groups)
-        up = dot(swap_w, up_ref[part, :]).astype(BF16)
-        for g in range(nt):
-            upp[g, b * step : (b + 1) * step, :] = up[g * step : (g + 1) * step, :]
-        down = dot(swap_w, down_ref[part, :]).astype(BF16)
-        for g in range(groups):
-            downp[0, b * step : (b + 1) * step, g * 128 : (g + 1) * 128] = down[g * step : (g + 1) * step, :]
-    upg[0, t] = upp[t]
+    for fetch in fetches[:4]:
+        fetch.wait()
+    att = attend(q_ref, k_ref, v_ref, len_ref[...].astype(F32), rows, groups, cache)
+    swap = regroup(rows, groups)
+    att = dot(swap, att).astype(BF16)
+    for g in range(groups):
+        xg[0:rows, g * 128 : (g + 1) * 128] = att[g * rows : (g + 1) * rows, :]
 
     pl.semaphore_wait(barrier, (nt - 1) + (nd - 1) + (na - 1))
-
-    def u_copy(k):
-        return pltpu.make_async_remote_copy(
-            src_ref=upp.at[lax.rem(t + k, nt)], dst_ref=upg.at[0, t], send_sem=u_send.at[k],
-            recv_sem=u_recv.at[k], device_id=z_dev(k), device_id_type=MESH)
-
-    def u_arrival(k):
-        return pltpu.make_async_remote_copy(
-            src_ref=upp.at[lax.rem(t + k, nt)], dst_ref=upg.at[0, lax.rem(t - k + nt, nt)], send_sem=u_send.at[k],
-            recv_sem=u_recv.at[k], device_id=z_dev(k), device_id_type=MESH)
-
-    def beside_dev(side):
-        return (at_chip(1 if side == 1 else -1, 0), t, a)
-
-    def d_copy(side):
-        return pltpu.make_async_remote_copy(
-            src_ref=downp.at[0], dst_ref=downp.at[3 - side], send_sem=d_send.at[side],
-            recv_sem=d_recv.at[3 - side], device_id=beside_dev(side), device_id_type=MESH)
-
-    def v_copy(side, k):
-        block = lax.rem(t - k + nt, nt)
-        return pltpu.make_async_remote_copy(
-            src_ref=upg.at[0, block], dst_ref=upg.at[3 - side, block], send_sem=v_send.at[side, k],
-            recv_sem=v_recv.at[3 - side, k], device_id=beside_dev(side), device_id_type=MESH)
-
-    for side in (1, 2):
-        d_copy(side).start()
-        v_copy(side, 0).start()
-
-    for fetch in fetches[2:8]:
+    order_z = ring_order(nt)
+    pos_z = [order_z.index(k) for k in range(nt)]
+
+    def z_part(place):
+        return xg.at[pl.ds(place * rows, rows)]
+
+    def z_copy(place, hop, far):
+        return pltpu.make_async_remote_copy(
+            src_ref=z_part(place), dst_ref=z_part(pos_z[far]), send_sem=z_send.at[far], recv_sem=z_recv.at[far],
+            device_id=(d, lax.rem(t + hop + nt, nt), a), device_id_type=MESH)
+
+    def z_arrival(k):
+        return pltpu.make_async_remote_copy(
+            src_ref=z_part(0), dst_ref=z_part(pos_z[k]), send_sem=z_send.at[k], recv_sem=z_recv.at[k],
+            device_id=z_dev(k), device_id_type=MESH)
+
+    halfway = nt // 2
+    z_first = [(0, 2, 2), (0, -2, nt - 2), (0, 1, 1), (0, -1, nt - 1)]
+    z_second = [
+        (pos_z[2], 1, 3), (pos_z[nt - 2], -1, nt - 3),
+        (pos_z[2] + (pos_z[nt - 2] - pos_z[2]) * core, 2 - 4 * core, halfway)]
+    for copy in z_first:
+        z_copy(*copy).start()
+
+    for fetch in fetches[4:6]:
         fetch.wait()
     idx_col = column_of(idx_ref[...].astype(F32), rows)
     table = slot_ref.shape[1]
@@ -209,49 +206,88 @@
     lane = iota((rows, lanes), 1)
     tags = jnp.where(lane == 0, owner_col * CAP + pos_col, jnp.where(lane == 1, local_col, 0.0))
 
-    att = attend(q_ref, k_ref, v_ref, len_ref[...].astype(F32), rows, groups, cache)
-    swap = regroup(rows, groups)
-    att = dot(swap, att).astype(BF16)
-    mine = pl.ds(pl.multiple_of(t * rows, rows), rows)
-    for g in range(groups):
-        xg[mine, g * 128 : (g + 1) * 128] = att[g * rows : (g + 1) * rows, :]
-    xg[mine, feat : feat + lanes] = tags.astype(BF16)
-
-    def z_copy(k, hop):
+    tg[0:rows, :] = tags.astype(BF16)
+
+    def t_copy(k):
+        return pltpu.make_async_remote_copy(
+            src_ref=tg.at[pl.ds(0, rows)], dst_ref=tg.at[pl.ds(pos_z[k] * rows, rows)], send_sem=t_send.at[k],
+            recv_sem=t_recv.at[k], device_id=z_dev(k), device_id_type=MESH)
+    for k in order_z[1:]:
+        t_copy(k).start()
+
+    fetches[6].wait()
+    step = 256 // groups
+    swap_w = regroup(step, groups)
+    for b in range(holding * half // step):
+        part = slice(b * step * groups, (b + 1) * step * groups)
+        up = dot(swap_w, up_ref[part, :]).astype(BF16)
+        for g in range(nt):
+            upp[g, b * step : (b + 1) * step, :] = up[g * step : (g + 1) * step, :]
+    upg[0, t] = upp[t]
+
+    def u_copy(k):
+        return pltpu.make_async_remote_copy(
+            src_ref=upp.at[lax.rem(t + k, nt)], dst_ref=upg.at[0, t], send_sem=u_send.at[k],
+            recv_sem=u_recv.at[k], device_id=z_dev(k), device_id_type=MESH)
+
+    def u_arrival(k):
+        return pltpu.make_async_remote_copy(
+            src_ref=upp.at[lax.rem(t + k, nt)], dst_ref=upg.at[0, lax.rem(t - k + nt, nt)], send_sem=u_send.at[k],
+            recv_sem=u_recv.at[k], device_id=z_dev(k), device_id_type=MESH)
+
+    def beside_dev(side):
+        return (at_chip(1 if side == 1 else -1, 0), t, a)
+
+    def d_copy(side):
+        return pltpu.make_async_remote_copy(
+            src_ref=downp.at[0], dst_ref=downp.at[3 - side], send_sem=d_send.at[side],
+            recv_sem=d_recv.at[3 - side], device_id=beside_dev(side), device_id_type=MESH)
+
+    def v_copy(side, k):
         block = lax.rem(t - k + nt, nt)
-        part = xg.at[pl.ds(pl.multiple_of(block * rows, rows), rows)]
-        far = (k + hop) % nt
-        return pltpu.make_async_remote_copy(
-            src_ref=part, dst_ref=part, send_sem=z_send.at[far], recv_sem=z_recv.at[far],
-            device_id=z_dev(hop % nt), device_id_type=MESH)
-
-    def z_arrival(k):
-        block = lax.rem(t - k + nt, nt)
-        part = xg.at[pl.ds(pl.multiple_of(block * rows, rows), rows)]
-        return pltpu.make_async_remote_copy(
-            src_ref=part, dst_ref=part, send_sem=z_send.at[k], recv_sem=z_recv.at[k],
-            device_id=z_dev(k), device_id_type=MESH)
-
-    z_first = [(0, 2), (0, -2), (0, 1), (0, -1)]
-    z_second = {2: [(2, 2), (2, 1)], nt - 2: [(nt - 2, -1)]}
-    for k, hop in z_first:
-        z_copy(k, hop).start()
-    for k, copies in z_second.items():
-        z_arrival(k).wait_recv()
-        for block, hop in copies:
-            z_copy(block, hop).start()
-
-    for k in range(1, nt):
-        if k not in z_second:
-            z_arrival(k).wait_recv()
-
-    tag = xg[:, feat : feat + lanes].astype(F32)
+        return pltpu.make_async_remote_copy(
+            src_ref=upg.at[0, block], dst_ref=upg.at[3 - side, block], send_sem=v_send.at[side, k],
+            recv_sem=v_recv.at[3 - side, k], device_id=beside_dev(side), device_id_type=MESH)
+
+    for side in (1, 2):
+        v_copy(side, 0).start()
+    near_z = ring_order(nt)[1:]
+    early = 2
+    for k in near_z[:early]:
+        u_copy(k).start()
+
+    def hand_on(first, last):
+        for k in near_z[first:last]:
+            u_arrival(k).wait_recv()
+            for side in (1, 2):
+                v_copy(side, k).start()
+
+    fetches[7].wait()
+    for b in range(holding * half // step):
+        part = slice(b * step * groups, (b + 1) * step * groups)
+        down = dot(swap_w, down_ref[part, :]).astype(BF16)
+        for g in range(groups):
+            downp[0, b * step : (b + 1) * step, g * 128 : (g + 1) * 128] = down[g * step : (g + 1) * step, :]
+    for side in (1, 2):
+        d_copy(side).start()
+
+    z_arrival(2).wait_recv()
+    z_copy(*z_second[0]).start()
+    z_arrival(nt - 2).wait_recv()
+    z_copy(*z_second[1]).start()
+    z_copy(*z_second[2]).start()
+    hand_on(0, early)
+    for k in order_z[1:]:
+        t_copy(k).wait_recv()
+    tag = tg[...].astype(F32)
     codes, local = tag[:, 0:1], tag[:, 1:2]
     owners = jnp.floor(codes * (1.0 / CAP))
     pos = codes - CAP * owners
     owner_d = jnp.floor(owners * (1.0 / nt))
     owner_t = owners - nt * owner_d
-    place = (iota((all_rows, 1), 0) // rows).astype(F32) * CAP + pos
+    block = iota((all_rows, 1), 0) // rows
+    block = jnp.where(block % 2 == 1, (block + 1) // 2, nt - block // 2)
+    place = ((t - block + nt) % nt).astype(F32) * CAP + pos
     target = owner_d * spots + place
     target_row = row_of(target, all_rows)
     here_row = row_of(jnp.where(owner_t == t.astype(F32), 1.0, 0.0), all_rows)
@@ -260,9 +296,33 @@
     places = jnp.where((wide_lane - 8).astype(F32) == owner_t, local + 1.0, 0.0).astype(BF16)
     beside = dot(route.astype(BF16), places)
     route = (route * here_row).astype(BF16)
-    beside = beside + jnp.where(iota((slots, lanes), 1) == 1, dot(route, xg[:, feat : feat + lanes]), 0.0)
-    pk[:, :feat] = dot(route, xg[:, :feat]).astype(BF16)
+    beside = beside + jnp.where(iota((slots, lanes), 1) == 1, dot(route, tg[...]), 0.0)
     pk[:, feat : feat + lanes] = beside.astype(BF16)
+
+    z_arrival(1).wait_recv()
+    z_arrival(nt - 1).wait_recv()
+
+    fetches[8].wait()
+    near_rows = 5 * rows
+
+    def b_copy(k, h):
+        part = pl.ds(h * near_rows, near_rows if h == 0 else all_rows - near_rows)
+        return pltpu.make_async_remote_copy(
+            src_ref=btx.at[k, part], dst_ref=brx.at[k, part], send_sem=b_send.at[h, k],
+            recv_sem=b_recv.at[h, k], device_id=x_dev(k), device_id_type=MESH)
+
+    def project(h):
+        part = slice(0, near_rows) if h == 0 else slice(near_rows, all_rows)
+        x = xg[part, :]
+        for k in range(1, na):
+            at = pl.ds(pl.multiple_of(lax.rem(a + k, na) * cols, cols), cols)
+            btx[k, part, :] = dot(x, w_ref[:, at]).astype(BF16)
+            b_copy(k, h).start()
+        acc[part, :] = dot(x, w_ref[:, pl.ds(pl.multiple_of(a * cols, cols), cols)])
+    project(0)
+    for k in (3, nt - 3, halfway):
+        z_arrival(k).wait_recv()
+    pk[:, :feat] = dot(route, xg[...]).astype(BF16)
 
     def y_copy(m):
         return pltpu.make_async_remote_copy(
@@ -270,25 +330,13 @@
             dst_ref=rx.at[pl.ds(m * spots, spots)], send_sem=y_send.at[m],
             recv_sem=y_recv.at[m], device_id=(server_at(m), t, a), device_id_type=MESH)
 
-    own = [m for m in range(nd) if m % 2 == 0 and abs(near[m // 2]) < 2]
+    own = [m for m in range(nd) if m % 2 == 0 and abs(away(m)) < 2]
     others = [m for m in range(nd) if m not in own]
     for m in others:
         y_copy(m).start()
-    near_z = sorted(range(1, nt), key=lambda k: min(k, nt - k))
-    for k in near_z:
+    for k in near_z[early:]:
         u_copy(k).start()
 
-    def hand_on(first, last):
-        for k in near_z[first:last]:
-            u_arrival(k).wait_recv()
-            for side in (1, 2):
-                v_copy(side, k).start()
-
-    fetches[8].wait()
-    x = xg[:, :feat]
-    for k in range(1, na):
-        part = pl.ds(pl.multiple_of(lax.rem(a + k, na) * cols, cols), cols)
-        btx[k] = dot(x, w_ref[:, part]).astype(BF16)
     for m in own:
         rx[m * spots : (m + 1) * spots, :] = pk[pl.ds(pl.multiple_of(owner_at(m) * spots, spots), spots), :]
 
@@ -321,9 +369,6 @@
         for m in range(lo, hi):
             if m in others:
                 y_copy(m).wait_recv()
-        if c == 0:
-            for side in (1, 2):
-                d_copy(side).wait_recv()
         shrunk = jnp.concatenate(
             [dot_t(rx[first * spots : last * spots, :feat], downp[side]) for first, last, side in maps_of(lo, hi)], axis=0)
         at = iota((n, lanes), 1)
@@ -376,31 +421,28 @@
             if m in others:
                 f_copy(m).start()
 
-    def b_copy(k):
-        return pltpu.make_async_remote_copy(
-            src_ref=btx.at[k], dst_ref=brx.at[k], send_sem=b_send.at[k],
-            recv_sem=b_recv.at[k], device_id=x_dev(k), device_id_type=MESH)
-
-    s0 = down_of(0)
-    sum_of(0, s0)
-    hand_on(0, 2)
-    s1 = down_of(1)
-    hand_on(2, 4)
-    sum_of(1, s1)
-    s2 = down_of(2)
-    hand_on(4, 6)
-    sum_of(2, s2)
+    for side in (1, 2):
+        d_copy(side).wait_recv()
+    near_sum = down_of(0)
+    sum_of(0, near_sum)
+    hand_on(early, 4)
+    first_sum = down_of(1)
+    hand_on(4, 5)
+    sum_of(1, first_sum)
+    hand_on(5, 6)
+    next_sum = down_of(2)
     hand_on(6, nt)
-    for k in range(1, na):
-        b_copy(k).start()
+    sum_of(2, next_sum)
+    project(1)
     up_of(0)
     up_of(1)
     up_of(2)
     for m in own:
         ret_rx[m] = ret_tx[m]
-    acc[...] = dot(x, w_ref[:, pl.ds(pl.multiple_of(a * cols, cols), cols)])
+    for h in (0, 1):
+        for k in range(1, na):
+            b_copy(k, h).wait_recv()
     for k in range(1, na):
-        b_copy(k).wait_recv()
         acc[...] += brx[k].astype(F32)
 
     target = owners * spots + place
@@ -412,7 +454,9 @@
         place_of = (iota((all_rows, span), 1) + owner_at(m) * span).astype(F32)
         pick = jnp.where(place_of == target, 1.0, 0.0).astype(BF16)
         total = total + dot(pick, ret_rx[m].reshape(span, cols))
-    out_ref[...] = total.astype(BF16)
+    for k in range(nt):
+        out_ref[pl.ds(pl.multiple_of(lax.rem(t - k + nt, nt) * rows, rows), rows), :] = total[
+            pos_z[k] * rows : (pos_z[k] + 1) * rows].astype(BF16)
 
     def drain_z(k, c):
         u_copy(k).wait_send()
@@ -420,8 +464,8 @@
             r_copy(r, k, t).wait_send()
         return c
     lax.fori_loop(1, nt, drain_z, 0)
-    for k, hop in z_first + [copy for copies in z_second.values() for copy in copies]:
-        z_copy(k, hop).wait_send()
+    for copy in z_first + z_second:
+        z_copy(*copy).wait_send()
 
     def drain_v(k, c):
         for side in (1, 2):
@@ -430,11 +474,14 @@
     lax.fori_loop(0, nt, drain_v, 0)
     for side in (1, 2):
         d_copy(side).wait_send()
+    for k in order_z[1:]:
+        t_copy(k).wait_send()
     for m in others:
         y_copy(m).wait_send()
         f_copy(m).wait_send()
     for k in range(1, na):
-        b_copy(k).wait_send()
+        b_copy(k, 0).wait_send()
+        b_copy(k, 1).wait_send()
         for c in range(len(runs)):
             p_copy(c, k).wait_send()
 
@@ -467,7 +514,8 @@
             pltpu.VMEM((1, table.shape[0]), jnp.int32),
             pltpu.VMEM((hr * groups, width), BF16),
             pltpu.VMEM((hr * nt, cols), BF16),
-            pltpu.VMEM((nt * rows, wide), BF16),
+            pltpu.VMEM((nt * rows, feat), BF16),
+            pltpu.VMEM((nt * rows, hr), BF16),
             pltpu.VMEM((slots, wide), BF16),
             pltpu.VMEM((slots, wide), BF16),
             pltpu.VMEM((feat, columns), BF16),
@@ -485,10 +533,11 @@
             dma((9,)),
             dma((nt,)), dma((nt,)), dma((nt,)), dma((nt,)),
             dma((nd,)), dma((nd,)),
-            dma((na,)), dma((na,)), dma((parts, na)), dma((parts, na)),
+            dma((2, na)), dma((2, na)), dma((parts, na)), dma((parts, na)),
             dma((parts, nt)), dma((parts, nt)),
             dma((nd,)), dma((nd,)),
             dma((3,)), dma((3,)), dma((3, nt)), dma((3, nt)),
+            dma((nt,)), dma((nt,)),
         ],
         compiler_params=pltpu.CompilerParams(
             collective_id=0, has_side_effects=True, vmem_limit_bytes=60 * 1024 * 1024

time: 75.2 us -> 64.9 us (0.86)
  the two profiles are of different devices: /device:TPU:9 before, /device:TPU:1 now
where the time goes in v4:
time: 64.9 us; the launch traced here: 64.1 us
  Pallas kernels  62.5 us (96%)
  local copies, waits for them, and re-layouts  1.57 us (2%)
    pallas_call x1, Pallas kernels, body(): pl.pallas_call(functools.partial(kernel, nd, nt, na, groups, cache, holdi...  62.5 us
    unnamed x1, local copies, waits for them, and re-layouts  1.57 us

profile of v4, /device:TPU:1, one launch (start us, length us, event | category | flops | bytes accessed | tf_op | source)
XLA Modules:
  0.0 64.1 jit_solution(11583275297844897334)
XLA Ops:
  0.0 62.5 %shard_map.91 = bf16[256,256]{1,0:T(8,128)(2,1)} custom-call(bf16[256,128]{1,0:T(8,128)(2,1)} %bitcast.14, bf16[512,128]{1,0:T(8,128)(2,1)} %bitcast.12, bf16[512,128]{1,0:T(8,128)(2,1)} %bitcast.13, s32[1,32]{1,0:T(1,128)} %bitcast.16, s32[1,32]{1,0:T(1,128)} %bitcast.17, s32[1,256]{1,0:T(1,128)} %bitcast.15, bf16[1024,1024]{1,0:T(8,128)(2,1)} %bitcast.9, ...), custom_call_target="tpu_custom_call" | custom-call | tf_op jit(solution)/shard_map/pallas_call | solution.py:503
  62.5 1.6 %copy.11 = bf16[256,256]{1,0:T(8,128)(2,1)} copy(bf16[256,256]{1,0:T(8,128)(2,1)} %shard_map.91) | data formatting | bytes 262144

commit v5 on v4

--- a/solution.py
+++ b/solution.py
@@ -212,7 +212,7 @@
         return pltpu.make_async_remote_copy(
             src_ref=tg.at[pl.ds(0, rows)], dst_ref=tg.at[pl.ds(pos_z[k] * rows, rows)], send_sem=t_send.at[k],
             recv_sem=t_recv.at[k], device_id=z_dev(k), device_id_type=MESH)
-    for k in order_z[1:]:
+    for k in reversed(order_z[1:]):
         t_copy(k).start()
 
     fetches[6].wait()
@@ -446,6 +446,32 @@
         acc[...] += brx[k].astype(F32)
 
     target = owners * spots + place
+    def drain_z(k, c):
+        u_copy(k).wait_send()
+        for r in range(len(runs)):
+            r_copy(r, k, t).wait_send()
+        return c
+    lax.fori_loop(1, nt, drain_z, 0)
+    for copy in z_first + z_second:
+        z_copy(*copy).wait_send()
+
+    def drain_v(k, c):
+        for side in (1, 2):
+            v_copy(side, k).wait_send()
+        return c
+    lax.fori_loop(0, nt, drain_v, 0)
+    for side in (1, 2):
+        d_copy(side).wait_send()
+    for k in order_z[1:]:
+        t_copy(k).wait_send()
+    for m in others:
+        y_copy(m).wait_send()
+    for k in range(1, na):
+        b_copy(k, 0).wait_send()
+        b_copy(k, 1).wait_send()
+        for c in range(len(runs)):
+            p_copy(c, k).wait_send()
+
     total = acc[...]
     span = nt * spots
     for m in range(nd):
@@ -457,33 +483,8 @@
     for k in range(nt):
         out_ref[pl.ds(pl.multiple_of(lax.rem(t - k + nt, nt) * rows, rows), rows), :] = total[
             pos_z[k] * rows : (pos_z[k] + 1) * rows].astype(BF16)
-
-    def drain_z(k, c):
-        u_copy(k).wait_send()
-        for r in range(len(runs)):
-            r_copy(r, k, t).wait_send()
-        return c
-    lax.fori_loop(1, nt, drain_z, 0)
-    for copy in z_first + z_second:
-        z_copy(*copy).wait_send()
-
-    def drain_v(k, c):
-        for side in (1, 2):
-            v_copy(side, k).wait_send()
-        return c
-    lax.fori_loop(0, nt, drain_v, 0)
-    for side in (1, 2):
-        d_copy(side).wait_send()
-    for k in order_z[1:]:
-        t_copy(k).wait_send()
     for m in others:
-        y_copy(m).wait_send()
         f_copy(m).wait_send()
-    for k in range(1, na):
-        b_copy(k, 0).wait_send()
-        b_copy(k, 1).wait_send()
-        for c in range(len(runs)):
-            p_copy(c, k).wait_send()
 
 
 def body(sizes, q, kc, vc, lengths, index, table, w, down, up):

time: 64.9 us -> 64.7 us (level); the launches traced: 64.1 us -> 64.5 us
  no operation moved by 1% of the time
where the time goes in v5:
time: 64.7 us; the launch traced here: 64.5 us
  Pallas kernels  62.9 us (97%)
  local copies, waits for them, and re-layouts  1.57 us (2%)
    pallas_call x1, Pallas kernels, body(): pl.pallas_call(functools.partial(kernel, nd, nt, na, groups, cache, holdi...  62.9 us
    unnamed x1, local copies, waits for them, and re-layouts  1.57 us

profile of v5, /device:TPU:1, one launch (start us, length us, event | category | flops | bytes accessed | tf_op | source)
XLA Modules:
  0.0 64.5 jit_solution(9405886228785825339)
XLA Ops:
  0.0 62.9 %shard_map.91 = bf16[256,256]{1,0:T(8,128)(2,1)} custom-call(bf16[256,128]{1,0:T(8,128)(2,1)} %bitcast.14, bf16[512,128]{1,0:T(8,128)(2,1)} %bitcast.12, bf16[512,128]{1,0:T(8,128)(2,1)} %bitcast.13, s32[1,32]{1,0:T(1,128)} %bitcast.16, s32[1,32]{1,0:T(1,128)} %bitcast.17, s32[1,256]{1,0:T(1,128)} %bitcast.15, bf16[1024,1024]{1,0:T(8,128)(2,1)} %bitcast.9, ...), custom_call_target="tpu_custom_call" | custom-call | tf_op jit(solution)/shard_map/pallas_call | solution.py:504
  63.0 1.6 %copy.11 = bf16[256,256]{1,0:T(8,128)(2,1)} copy(bf16[256,256]{1,0:T(8,128)(2,1)} %shard_map.91) | data formatting | bytes 262144

commit v6 on v5

--- a/solution.py
+++ b/solution.py
@@ -387,10 +387,8 @@
             shrunk = shrunk + prx[k, packed(runs[c]), :].astype(F32)
         redg[t, packed(runs[c]), :] = shrunk.astype(BF16)
 
-        def r_start(k, s):
+        for k in reversed(order_z[1:]):
             r_copy(c, k, t).start()
-            return s
-        lax.fori_loop(1, nt, r_start, 0)
 
     def up_of(c):
         lo, hi = runs[c]
@@ -424,8 +422,8 @@
     for side in (1, 2):
         d_copy(side).wait_recv()
     near_sum = down_of(0)
+    hand_on(early, 4)
     sum_of(0, near_sum)
-    hand_on(early, 4)
     first_sum = down_of(1)
     hand_on(4, 5)
     sum_of(1, first_sum)

time: 64.7 us -> 64.8 us (level)
  no operation moved by 1% of the time
where the time goes in v6:
time: 64.8 us; the launch traced here: 64.4 us
  Pallas kernels  62.8 us (97%)
  local copies, waits for them, and re-layouts  1.57 us (2%)
    pallas_call x1, Pallas kernels, body(): pl.pallas_call(functools.partial(kernel, nd, nt, na, groups, cache, holdi...  62.8 us
    unnamed x1, local copies, waits for them, and re-layouts  1.57 us

profile of v6, /device:TPU:1, one launch (start us, length us, event | category | flops | bytes accessed | tf_op | source)
XLA Modules:
  0.0 64.4 jit_solution(15860853155164700841)
XLA Ops:
  0.0 62.8 %shard_map.91 = bf16[256,256]{1,0:T(8,128)(2,1)} custom-call(bf16[256,128]{1,0:T(8,128)(2,1)} %bitcast.14, bf16[512,128]{1,0:T(8,128)(2,1)} %bitcast.12, bf16[512,128]{1,0:T(8,128)(2,1)} %bitcast.13, s32[1,32]{1,0:T(1,128)} %bitcast.16, s32[1,32]{1,0:T(1,128)} %bitcast.17, s32[1,256]{1,0:T(1,128)} %bitcast.15, bf16[1024,1024]{1,0:T(8,128)(2,1)} %bitcast.9, ...), custom_call_target="tpu_custom_call" | custom-call | tf_op jit(solution)/shard_map/pallas_call | solution.py:502
  62.8 1.6 %copy.11 = bf16[256,256]{1,0:T(8,128)(2,1)} copy(bf16[256,256]{1,0:T(8,128)(2,1)} %shard_map.91) | data formatting | bytes 262144
